TPU v7x, 32 devices: a whole 2x2x4 slice. The times are simulated.
32 devices in a mesh: dp: 16 (over z, y, x), mp: 2 (over core).
Axes of the slice: x: 2, y: 2, z: 4, core: 2. Of those that a mesh axis runs over, the one named last changes fastest.
Arguments:
- tokens: bfloat16 [2, 16384, 768], P(None, 'dp', 'mp'), may hold values from -7.5 to 7.5, as said below
- cotangent: bfloat16 [2, 16384, 768], P(None, 'dp', 'mp'), may hold values from -6 to 6
- segments: int32 [2, 16, 1024], P(None, 'dp'), may hold values from 0 to 3, never falling along the last dimension, each value on 1 to 512 neighbouring positions
- head_gates: int32 [12], P('mp'), may hold values 0 or 1
- unit_gates: int32 [3072], P('mp'), may hold values 0 or 1
- hidden_gates: int32 [768], P('mp'), may hold values 0 or 1
- layer_gates: float32 [2], replicated, may hold values from 0.5 to 1
- w_qkv: float32 [3, 768, 768], P(None, 'dp', 'mp'), may hold values from -0.21875 to 0.21875
- w_out: float32 [768, 768], P('mp', 'dp'), may hold values from -0.875 to 0.875
- w_in: float32 [768, 3072], P('dp', 'mp'), may hold values from -0.21875 to 0.21875
- w_back: float32 [3072, 768], P('mp', 'dp'), may hold values from -0.109375 to 0.109375
- norm_params: float32 [4, 768], P(None, 'mp'), may hold values from -1 to 3.2, as said below
- mom_qkv: float32 [3, 768, 768], P(None, 'dp', 'mp'), may hold values from -0.00061035156 to 0.00061035156
- mom_out: float32 [768, 768], P('mp', 'dp'), may hold values from -0.00061035156 to 0.00061035156
- mom_in: float32 [768, 3072], P('dp', 'mp'), may hold values from -0.00061035156 to 0.00061035156
- mom_back: float32 [3072, 768], P('mp', 'dp'), may hold values from -0.00061035156 to 0.00061035156
- mom_norm: float32 [4, 768], P(None, 'mp'), may hold values from -0.00061035156 to 0.00061035156
- sec_qkv: float32 [3, 768, 768], P(None, 'dp', 'mp'), may hold values from 7.061189e-11 to 1.1297903e-09
- sec_out: float32 [768, 768], P('mp', 'dp'), may hold values from 7.061189e-11 to 1.1297903e-09
- sec_in: float32 [768, 3072], P('dp', 'mp'), may hold values from 7.061189e-11 to 1.1297903e-09
- sec_back: float32 [3072, 768], P('mp', 'dp'), may hold values from 7.061189e-11 to 1.1297903e-09
- sec_norm: float32 [4, 768], P(None, 'mp'), may hold values from 7.061189e-11 to 1.1297903e-09
Outputs:
- out_tokens: bfloat16 [2, 16384, 768], P(None, 'dp', 'mp')
- input_grad: bfloat16 [2, 16384, 768], P(None, 'dp', 'mp')
- grad_norm: float32 [], replicated
- new_w_qkv: float32 [3, 768, 768], P(None, 'dp', 'mp')
- new_w_out: float32 [768, 768], P('mp', 'dp')
- new_w_in: float32 [768, 3072], P('dp', 'mp')
- new_w_back: float32 [3072, 768], P('mp', 'dp')
- new_norm: float32 [4, 768], P(None, 'mp')
- new_m_qkv: float32 [3, 768, 768], P(None, 'dp', 'mp')
- new_m_out: float32 [768, 768], P('mp', 'dp')
- new_m_in: float32 [768, 3072], P('dp', 'mp')
- new_m_back: float32 [3072, 768], P('mp', 'dp')
- new_m_norm: float32 [4, 768], P(None, 'mp')
- new_v_qkv: float32 [3, 768, 768], P(None, 'dp', 'mp')
- new_v_out: float32 [768, 768], P('mp', 'dp')
- new_v_in: float32 [768, 3072], P('dp', 'mp')
- new_v_back: float32 [3072, 768], P('mp', 'dp')
- new_v_norm: float32 [4, 768], P(None, 'mp')
Inputs may be any that keep to these rules, and one draw needn't show every extreme that they name: `segments`: within each packed sequence of 1024 positions the ids never fall; a document has at most 512 positions, and one has exactly that many. `tokens`: entries of order one. `norm_params`: gains are positive.
All inputs are finite; a program needn't handle non-finite values. No bound on the sum of `head_gates` or of `unit_gates` or of `hidden_gates` on one device may be relied on, other than what follows from the above.
Results may differ from a plain program's by a relative error of at most 0.0098.
Values may be sent and summed in bfloat16 or wider, within the bound.
No kernel may reach another device: no remote copies, remote signals or barrier semaphores. Data moves between devices by JAX's collectives and lax.ppermute only.
A program may use at most 192 MiB of HBM per device.

v0:
```python
import jax
import jax.numpy as jnp
from jax import lax
from jax.sharding import PartitionSpec as P

D = 768
HEAD_DIM = 64
MICRO = 2
BLOCK = 512
STEP = 10


LN_EPS = 1e-12
NEG_FILL = -1000000000.0
CLIP_NORM = 1.0
LEARN_RATE = 0.06
NORM_RATE = 0.3
WEIGHT_DECAY = 0.01
BETA_ONE = 0.9
BETA_TWO = 0.999
ADAM_EPS = 1e-08
CONTRACT_LAST = (((1,), (1,)), ((), ()))
CONTRACT_FIRST = (((0,), (0,)), ((), ()))


def gelu_exact(values):
    return jax.nn.gelu(values, approximate=False)


def norm_forward(residual, gain_vec, shift_vec):
    totals = lax.psum((jnp.sum(residual, axis=-1), jnp.sum(residual * residual, axis=-1)), "mp")
    mean_val = totals[0][:, None] / D
    var_val = totals[1][:, None] / D - mean_val * mean_val
    inv_std = lax.rsqrt(var_val + LN_EPS)
    centred = (residual - mean_val) * inv_std
    return (centred * gain_vec + shift_vec, centred, inv_std)


def norm_backward(grad_out, centred, inv_std, gain_vec):
    scaled = grad_out * gain_vec
    totals = lax.psum((jnp.sum(scaled, axis=-1), jnp.sum(scaled * centred, axis=-1)), "mp")
    grad_in = inv_std * (scaled - totals[0][:, None] / D - centred * (totals[1][:, None] / D))
    return (grad_in, jnp.sum(grad_out * centred, axis=0), jnp.sum(grad_out, axis=0))


def block_scores(query_blk, seg_blk, keys_all, segment):
    scores = jnp.einsum(
        "qhc,khc->hqk", query_blk, keys_all, preferred_element_type=jnp.float32
    ) * HEAD_DIM ** (-0.5)
    allowed = seg_blk[:, None] == segment[None, :]
    return jnp.where(allowed[None], scores, NEG_FILL)


def attend_forward(queries, keys_all, values_all, segment):
    row_count, heads_here, head_width = queries.shape
    blocks = row_count // BLOCK

    def one_block(block_pair):
        scores = block_scores(block_pair[0], block_pair[1], keys_all, segment)
        top_val = jnp.max(scores, axis=-1, keepdims=True)
        expo_vals = jnp.exp(scores - top_val)
        denom_sum = jnp.sum(expo_vals, axis=-1, keepdims=True)
        prob_low = (expo_vals / denom_sum).astype(jnp.bfloat16)
        context = jnp.einsum(
            "hqk,khc->qhc", prob_low, values_all, preferred_element_type=jnp.float32
        )
        return (context, (top_val + jnp.log(denom_sum))[..., 0])

    context, log_sums = lax.map(
        one_block,
        (queries.reshape(blocks, BLOCK, heads_here, head_width), segment.reshape(blocks, BLOCK)),
    )
    return (context.reshape(row_count, heads_here, head_width), log_sums)


def attend_backward(queries, keys_all, values_all, segment, log_sums, grad_ctx):
    row_count, heads_here, head_width = queries.shape
    blocks = row_count // BLOCK
    attn_scale = HEAD_DIM ** (-0.5)

    def one_block(carry_sums, block_item):
        grad_keys, grad_vals = carry_sums
        query_blk, seg_blk, lse_blk, dctx_blk = block_item
        scores = block_scores(query_blk, seg_blk, keys_all, segment)
        attn_prob = jnp.exp(scores - lse_blk[..., None])
        prob_low = attn_prob.astype(jnp.bfloat16)
        grad_vals = grad_vals + jnp.einsum(
            "hqk,qhc->khc", prob_low, dctx_blk, preferred_element_type=jnp.float32
        )
        grad_prob = jnp.einsum(
            "qhc,khc->hqk", dctx_blk, values_all, preferred_element_type=jnp.float32
        )
        grad_score = attn_prob * (
            grad_prob - jnp.sum(attn_prob * grad_prob, axis=-1, keepdims=True)
        )
        score_low = grad_score.astype(jnp.bfloat16)
        grad_query = (
            jnp.einsum("hqk,khc->qhc", score_low, keys_all, preferred_element_type=jnp.float32)
            * attn_scale
        )
        grad_keys = (
            grad_keys
            + jnp.einsum("hqk,qhc->khc", score_low, query_blk, preferred_element_type=jnp.float32)
            * attn_scale
        )
        return ((grad_keys, grad_vals), grad_query)

    zero_rows = jnp.zeros((row_count, heads_here, head_width), jnp.float32)
    block_items = (
        queries.reshape(blocks, BLOCK, heads_here, head_width),
        segment.reshape(blocks, BLOCK),
        log_sums,
        grad_ctx.reshape(blocks, BLOCK, heads_here, head_width),
    )
    (grad_keys, grad_vals), grad_query = lax.scan(one_block, (zero_rows, zero_rows), block_items)
    return (grad_query.reshape(row_count, heads_here, head_width), grad_keys, grad_vals)


def adam_step(weight, gradient, first_mom, second, step_rate, decay_rate):
    first_new = BETA_ONE * first_mom + (1.0 - BETA_ONE) * gradient
    second_new = BETA_TWO * second + (1.0 - BETA_TWO) * gradient * gradient
    update = (
        first_new
        / (1.0 - BETA_ONE**STEP)
        / (jnp.sqrt(second_new / (1.0 - BETA_TWO**STEP)) + ADAM_EPS)
    )
    return (weight - step_rate * (update + decay_rate * weight), first_new, second_new)


def gather_weights(w_qkv, w_out, w_in, w_back):
    return (
        lax.all_gather(w_qkv.astype(jnp.bfloat16), "dp", axis=1, tiled=True),
        lax.all_gather(w_out.astype(jnp.bfloat16), "dp", axis=1, tiled=True),
        lax.all_gather(w_in.astype(jnp.bfloat16), "dp", axis=0, tiled=True),
        lax.all_gather(w_back.astype(jnp.bfloat16), "dp", axis=1, tiled=True),
    )


def scatter_grads(grad_set):
    return (
        lax.psum_scatter(grad_set[0], "dp", scatter_dimension=1, tiled=True),
        lax.psum_scatter(grad_set[1], "dp", scatter_dimension=1, tiled=True),
        lax.psum_scatter(grad_set[2], "dp", scatter_dimension=0, tiled=True),
        lax.psum_scatter(grad_set[3], "dp", scatter_dimension=1, tiled=True),
    )


def shards(
    tokens,
    cotangent,
    segments,
    head_gates,
    unit_gates,
    hidden_gates,
    layer_gates,
    w_qkv,
    w_out,
    w_in,
    w_back,
    norm_params,
    mom_qkv,
    mom_out,
    mom_in,
    mom_back,
    mom_norm,
    sec_qkv,
    sec_out,
    sec_in,
    sec_back,
    sec_norm,
):
    head_mask = head_gates.astype(jnp.float32)
    unit_mask = unit_gates.astype(jnp.float32)
    hidden_mask = hidden_gates.astype(jnp.float32)
    heads_here = head_gates.shape[0]
    gate_attn = layer_gates[0]
    gate_ffn = layer_gates[1]
    out_list = []
    grad_list = []
    shard_list = []
    norm_rows = jnp.zeros(norm_params.shape, jnp.float32)
    for micro_idx in range(MICRO):
        full_qkv, full_out, full_in, full_back = gather_weights(w_qkv, w_out, w_in, w_back)
        tok_here = tokens[micro_idx]
        segment = segments[micro_idx, 0]
        row_count = tok_here.shape[0]
        tok_full = lax.all_gather(tok_here, "mp", axis=1, tiled=True)
        qkv_low = jnp.einsum(
            "rd,tde->tre", tok_full, full_qkv, preferred_element_type=jnp.float32
        ).astype(jnp.bfloat16)
        queries = qkv_low[0].reshape(row_count, heads_here, HEAD_DIM)
        keys_all = qkv_low[1].reshape(row_count, heads_here, HEAD_DIM)
        values_all = qkv_low[2].reshape(row_count, heads_here, HEAD_DIM)
        context, log_sums = attend_forward(queries, keys_all, values_all, segment)
        gated_low = (context * head_mask[None, :, None]).reshape(row_count, -1).astype(jnp.bfloat16)
        attn_val = lax.psum_scatter(
            jnp.dot(gated_low, full_out, preferred_element_type=jnp.float32),
            "mp",
            scatter_dimension=1,
            tiled=True,
        )
        resid_one = tok_here.astype(jnp.float32) + gate_attn * attn_val * hidden_mask
        normed, centred_one, inv_one = norm_forward(resid_one, norm_params[0], norm_params[1])
        normed_full = lax.all_gather(normed.astype(jnp.bfloat16), "mp", axis=1, tiled=True)
        pre_act = jnp.dot(normed_full, full_in, preferred_element_type=jnp.float32)
        act_vals, gelu_back = jax.vjp(gelu_exact, pre_act)
        hidden_low = (act_vals * unit_mask).astype(jnp.bfloat16)
        ffn_val = lax.psum_scatter(
            jnp.dot(hidden_low, full_back, preferred_element_type=jnp.float32),
            "mp",
            scatter_dimension=1,
            tiled=True,
        )
        resid_two = normed + gate_ffn * ffn_val * hidden_mask
        result, centred_two, inv_two = norm_forward(resid_two, norm_params[2], norm_params[3])
        out_list.append(result.astype(jnp.bfloat16))
        grad_out = cotangent[micro_idx].astype(jnp.float32)
        grad_two, dgain_two, dshift_two = norm_backward(
            grad_out, centred_two, inv_two, norm_params[2]
        )
        grad_ffn = (gate_ffn * hidden_mask * grad_two).astype(jnp.bfloat16)
        grad_ffn_full = lax.all_gather(grad_ffn, "mp", axis=1, tiled=True)
        grad_hidden = lax.dot_general(
            grad_ffn_full, full_back, CONTRACT_LAST, preferred_element_type=jnp.float32
        )
        grad_wb = lax.dot_general(
            hidden_low, grad_ffn_full, CONTRACT_FIRST, preferred_element_type=jnp.float32
        )
        grad_pre = gelu_back(grad_hidden * unit_mask)[0].astype(jnp.bfloat16)
        grad_norm_part = lax.dot_general(
            grad_pre, full_in, CONTRACT_LAST, preferred_element_type=jnp.float32
        )
        grad_wi = lax.dot_general(
            normed_full, grad_pre, CONTRACT_FIRST, preferred_element_type=jnp.float32
        )
        grad_normed = grad_two + lax.psum_scatter(
            grad_norm_part, "mp", scatter_dimension=1, tiled=True
        )
        grad_one, dgain_one, dshift_one = norm_backward(
            grad_normed, centred_one, inv_one, norm_params[0]
        )
        grad_attn = (gate_attn * hidden_mask * grad_one).astype(jnp.bfloat16)
        grad_attn_full = lax.all_gather(grad_attn, "mp", axis=1, tiled=True)
        grad_gated = lax.dot_general(
            grad_attn_full, full_out, CONTRACT_LAST, preferred_element_type=jnp.float32
        )
        grad_wo = lax.dot_general(
            gated_low, grad_attn_full, CONTRACT_FIRST, preferred_element_type=jnp.float32
        )
        grad_ctx = (
            grad_gated.reshape(row_count, heads_here, HEAD_DIM) * head_mask[None, :, None]
        ).astype(jnp.bfloat16)
        grad_query, grad_keys, grad_vals = attend_backward(
            queries, keys_all, values_all, segment, log_sums, grad_ctx
        )
        grad_qkv = jnp.stack(
            [
                grad_query.reshape(row_count, -1),
                grad_keys.reshape(row_count, -1),
                grad_vals.reshape(row_count, -1),
            ]
        ).astype(jnp.bfloat16)
        grad_tok_part = jnp.einsum(
            "tre,tde->rd", grad_qkv, full_qkv, preferred_element_type=jnp.float32
        )
        grad_wq = jnp.einsum("rd,tre->tde", tok_full, grad_qkv, preferred_element_type=jnp.float32)
        grad_tok = grad_one + lax.psum_scatter(grad_tok_part, "mp", scatter_dimension=1, tiled=True)
        grad_list.append(grad_tok.astype(jnp.bfloat16))
        norm_rows = norm_rows + jnp.stack([dgain_one, dshift_one, dgain_two, dshift_two])
        shard_list.append(scatter_grads((grad_wq, grad_wo, grad_wi, grad_wb)))
    shard_sums = shard_list[0]
    for shard_set in shard_list[1:]:
        shard_sums = tuple((summed + extra for summed, extra in zip(shard_sums, shard_set)))
    norm_total = lax.psum(norm_rows, "dp")
    part_square = jnp.sum(norm_total * norm_total) / lax.axis_size("dp")
    for shard in shard_sums:
        part_square = part_square + jnp.sum(shard * shard)
    total_square = lax.psum(part_square, ("dp", "mp"))
    grad_norm = jnp.sqrt(total_square)
    factor = jnp.minimum(1.0, CLIP_NORM / grad_norm)
    weights = (w_qkv, w_out, w_in, w_back, norm_params)
    gradients = (shard_sums[0], shard_sums[1], shard_sums[2], shard_sums[3], norm_total)
    firsts = (mom_qkv, mom_out, mom_in, mom_back, mom_norm)
    seconds = (sec_qkv, sec_out, sec_in, sec_back, sec_norm)
    results = []
    for index in range(5):
        step_rate = LEARN_RATE if index < 4 else NORM_RATE
        decay_rate = WEIGHT_DECAY if index < 4 else 0.0
        results.append(
            adam_step(
                weights[index],
                gradients[index] * factor,
                firsts[index],
                seconds[index],
                step_rate,
                decay_rate,
            )
        )
    return (
        jnp.stack(out_list),
        jnp.stack(grad_list),
        grad_norm,
        results[0][0],
        results[1][0],
        results[2][0],
        results[3][0],
        results[4][0],
        results[0][1],
        results[1][1],
        results[2][1],
        results[3][1],
        results[4][1],
        results[0][2],
        results[1][2],
        results[2][2],
        results[3][2],
        results[4][2],
    )


def solution(mesh):
    in_specs = (
        P(None, "dp", "mp"),
        P(None, "dp", "mp"),
        P(None, "dp", None),
        P("mp"),
        P("mp"),
        P("mp"),
        P(),
        P(None, "dp", "mp"),
        P("mp", "dp"),
        P("dp", "mp"),
        P("mp", "dp"),
        P(None, "mp"),
        P(None, "dp", "mp"),
        P("mp", "dp"),
        P("dp", "mp"),
        P("mp", "dp"),
        P(None, "mp"),
        P(None, "dp", "mp"),
        P("mp", "dp"),
        P("dp", "mp"),
        P("mp", "dp"),
        P(None, "mp"),
    )
    out_specs = (
        P(None, "dp", "mp"),
        P(None, "dp", "mp"),
        P(),
        P(None, "dp", "mp"),
        P("mp", "dp"),
        P("dp", "mp"),
        P("mp", "dp"),
        P(None, "mp"),
        P(None, "dp", "mp"),
        P("mp", "dp"),
        P("dp", "mp"),
        P("mp", "dp"),
        P(None, "mp"),
        P(None, "dp", "mp"),
        P("mp", "dp"),
        P("dp", "mp"),
        P("mp", "dp"),
        P(None, "mp"),
    )
    return jax.shard_map(shards, mesh=mesh, in_specs=in_specs, out_specs=out_specs, check_vma=False)
```

profile of v0, /device:TPU:0, one launch (start us, length us, event | category | flops | bytes accessed | tf_op | source)
XLA Modules:
  0.0 1202.8 jit_solution(10241014750715152723)
XLA Ops:
  11.8 48.7 %all_gather.42 = bf16[384,768]{0,1:T(8,128)(2,1)} all-gather(bf16[384,48]{0,1:T(8,128)(2,1)S(1)} %convert_element_type.137), channel_id=1, replica_groups=mesh['dp'=16,'mp'=2] {'dp'}, dimensions={1}, use_global_device_ids=true | all-gather | bytes 626688 | tf_op jit(solution)/shard_map/all_gather | solution.py:133
  60.5 25.8 %all-gather.14.cloned.1.call-done = bf16[3,768,384]{2,1,0:T(8,128)(2,1)} async-done(((bf16[3,48,384]{2,1,0:T(8,128)(2,1)}), bf16[3,768,384]{2,1,0:T(8,128)(2,1)}) %all-gather.14.cloned.1.call-update) | async-done | bytes 1769488 | tf_op jit(solution)/shard_map/all_gather | solution.py:132
  94.9 52.2 %while.55 = (s32[]{:T(128)}, f32[2,512,6,64]{1,0,3,2:T(2,128)}, f32[2,6,512]{2,1,0:T(8,128)S(1)}, s32[2,512]{1,0:T(2,128)S(1)}, s32[1,1,1024]{2,1,0:T(1,128)S(1)...) while((s32[]{:T(128)}, f32[2,512,6,64]{1,0,3,2:T(2,128)}, ...), condition=%wide.region_17.18_spmd, body=%wide.region_14.17_spmd.sunk | while | flops 843576320 | bytes 45865076 | solution.py:69
  106.0 15.0 %dynamic_update_slice.35 = f32[2,512,6,64]{1,0,3,2:T(2,128)} dynamic-update-slice(f32[2,512,6,64]{1,0,3,2:T(2,128)} %get-tuple-element.1005, f32[1,512,6,64]{1,0,3,2:T(1,128)S(1)} %copy.187, s32[]{:T(128)} %get-tuple-element.1004, s32[]{:T(128)} %constant.52.clone.1..sunk.1, s32[]{:T(128)} %constant.52.clone.1..sunk.1, s32[]{:T(128)} %constant.52.clone.1..sunk.1) | dynamic-update-slice | bytes 1572868 | tf_op jit(solution)/shard_map/while/body/jit(dynamic_update_index_in_dim)/dynamic_update_slice | solution.py:69
  132.1 15.0 %dynamic_update_slice.35 = f32[2,512,6,64]{1,0,3,2:T(2,128)} dynamic-update-slice(f32[2,512,6,64]{1,0,3,2:T(2,128)} %get-tuple-element.1005, f32[1,512,6,64]{1,0,3,2:T(1,128)S(1)} %copy.187, s32[]{:T(128)} %get-tuple-element.1004, s32[]{:T(128)} %constant.52.clone.1..sunk.1, s32[]{:T(128)} %constant.52.clone.1..sunk.1, s32[]{:T(128)} %constant.52.clone.1..sunk.1) | dynamic-update-slice | bytes 1572868 | tf_op jit(solution)/shard_map/while/body/jit(dynamic_update_index_in_dim)/dynamic_update_slice | solution.py:69
  163.7 53.4 %while.54 = (s32[]{:T(128)}, f32[2,512,6,64]{1,0,3,2:T(2,128)}, f32[2,6,512]{2,1,0:T(8,128)}, s32[2,512]{1,0:T(2,128)S(1)}, s32[1,1,1024]{2,1,0:T(1,128)S(1)}, /...) while((s32[]{:T(128)}, f32[2,512,6,64]{1,0,3,2:T(2,128)}, ...), condition=%wide.region_3.4_spmd, body=%wide.region_0.3_spmd.sunk | while | flops 843576320 | bytes 45857392 | solution.py:69
  175.4 15.0 %dynamic_update_slice.33 = f32[2,512,6,64]{1,0,3,2:T(2,128)} dynamic-update-slice(f32[2,512,6,64]{1,0,3,2:T(2,128)} %get-tuple-element.975, f32[1,512,6,64]{1,0,3,2:T(1,128)S(1)} %copy.186, s32[]{:T(128)} %get-tuple-element.974, s32[]{:T(128)} %constant.52.clone.1..sunk, s32[]{:T(128)} %constant.52.clone.1..sunk, s32[]{:T(128)} %constant.52.clone.1..sunk) | dynamic-update-slice | bytes 1572868 | tf_op jit(solution)/shard_map/while/body/jit(dynamic_update_index_in_dim)/dynamic_update_slice | solution.py:69
  202.1 15.0 %dynamic_update_slice.33 = f32[2,512,6,64]{1,0,3,2:T(2,128)} dynamic-update-slice(f32[2,512,6,64]{1,0,3,2:T(2,128)} %get-tuple-element.975, f32[1,512,6,64]{1,0,3,2:T(1,128)S(1)} %copy.186, s32[]{:T(128)} %get-tuple-element.974, s32[]{:T(128)} %constant.52.clone.1..sunk, s32[]{:T(128)} %constant.52.clone.1..sunk, s32[]{:T(128)} %constant.52.clone.1..sunk) | dynamic-update-slice | bytes 1572868 | tf_op jit(solution)/shard_map/while/body/jit(dynamic_update_index_in_dim)/dynamic_update_slice | solution.py:69
  226.9 6.9 reduce-scatter.12.cloned.1.call-done
  244.5 56.1 %all-gather.18.cloned.1.call-done = bf16[768,1536]{1,0:T(8,128)(2,1)} async-done(((bf16[48,1536]{1,0:T(8,128)(2,1)}), bf16[768,1536]{1,0:T(8,128)(2,1)}) %all-gather.18.cloned.1.call-update) | async-done | bytes 2359312 | tf_op jit(solution)/shard_map/all_gather | solution.py:134
  300.5 10.7 all-gather.22.cloned.1.call-done
  311.3 7.4 fusion.141
  318.6 5.7 all-gather.16.cloned.1.call-done
  324.3 32.7 %multiply_convert_fusion.3 = (bf16[1024,1536]{1,0:T(8,128)(2,1)}, f32[1024,1536]{1,0:T(8,128)}, bf16[1024,1536]{1,0:T(8,128)(2,1)}, f32[1024,1536]{1,0:T(8,128)}, f32[1024,1536]{1,0:T(8,128)}) fusion(f32[1536]{0:T(1024)S(1)} %convert_element_type.141, f32[1024,1536]{1,0:T(8,128)} %fusion.141, bf16[1024,768]{1,0:T(8,128)(2,1)} %all-gather.16.cloned.1.call-done, ...), kind=kOutput, calls=%fused_computation.111 | convolution fusion | flops 2623537152 | bytes 35395584 | tf_op jit(solution)/shard_map/dot_general | solution.py:205
  357.0 34.2 %all-gather.20.cloned.1.call-done = bf16[1536,768]{0,1:T(8,128)(2,1)} async-done(((bf16[1536,48]{0,1:T(8,128)(2,1)}), bf16[1536,768]{0,1:T(8,128)(2,1)}) %all-gather.20.cloned.1.call-update) | async-done | bytes 2359312 | tf_op jit(solution)/shard_map/all_gather | solution.py:135
  391.2 6.9 fusion.140
  398.2 7.0 fusion.142
  408.0 14.4 %reduce-scatter.18.cloned.1.call-done = f32[1024,384]{1,0:T(8,128)} async-done(((f32[1024,768]{1,0:T(8,128)}), f32[1024,384]{1,0:T(8,128)}) %reduce-scatter.18.cloned.1.call-update) | async-done | bytes 1572880 | tf_op jit(solution)/shard_map/reduce_scatter | solution.py:208
  443.8 10.3 all-gather.24.cloned.1.call-done
  454.1 10.1 add_convert_fusion.1
  470.3 10.1 add_convert_fusion
  491.8 6.9 reduce-scatter.24.cloned.1.call-done
  506.6 5.4 multiply_convert_fusion.8
  512.7 5.2 fusion.148
  557.2 66.1 %while.56 = (s32[]{:T(128)}, f32[1024,6,64]{0,2,1:T(8,128)}, f32[1024,6,64]{0,2,1:T(8,128)}, bf16[2,512,6,64]{1,3,2,0:T(8,128)(2,1)}, bf16[2,512,6,64]{1,3,2,0:T...) while((s32[]{:T(128)}, f32[1024,6,64]{0,2,1:T(8,128)}, ...), condition=%wide.region_39.40_spmd.clone, body=%wide.region_37.39_spmd.clone.sunk | while | flops 2063135744 | bytes 211390704 | solution.py:115
  561.4 6.3 multiply_reduce_fusion.19
  567.7 5.1 multiply_convert_fusion.18
  572.8 5.6 bitcast_add_fusion.8
  578.4 6.4 fusion.251
  593.6 6.3 multiply_reduce_fusion.19
  605.0 6.0 bitcast_add_fusion.8
  610.9 6.3 fusion.251
  617.3 6.0 bitcast_add_fusion.9
  624.3 63.9 %while.57 = (s32[]{:T(128)}, f32[1024,6,64]{0,2,1:T(8,128)}, f32[1024,6,64]{0,2,1:T(8,128)}, bf16[2,512,6,64]{1,3,2,0:T(8,128)(2,1)}, bf16[2,512,6,64]{1,3,2,0:T...) while((s32[]{:T(128)}, f32[1024,6,64]{0,2,1:T(8,128)}, ...), condition=%wide.region_52.53_spmd.clone, body=%wide.region_50.52_spmd.clone.sunk | while | flops 2063135744 | bytes 217681712 | solution.py:115
  628.1 5.6 multiply_reduce_fusion.20
  638.8 5.8 bitcast_add_fusion.10
  644.6 6.3 fusion.262
  659.2 5.7 multiply_reduce_fusion.20
  669.9 5.8 bitcast_add_fusion.10
  675.7 6.4 fusion.262
  682.1 6.0 bitcast_add_fusion.11
  714.6 5.4 convolution_bitcast_fusion.1
  721.6 5.4 convolution_bitcast_fusion
  730.1 42.8 %psum.142 = f32[4,384]{1,0:T(4,128)S(1)} all-reduce(f32[4,384]{1,0:T(4,128)S(1)} %maximum_add_fusion), channel_id=1, replica_groups=mesh['dp'=16,'mp'=2] {'dp'}, use_global_device_ids=true, to_apply=%region_62.63 | all-reduce | flops 1536 | bytes 12288 | tf_op jit(solution)/shard_map/psum | solution.py:274
  775.9 46.7 %reduce-scatter.30.cloned.1.call-done = f32[48,1536]{1,0:T(8,128)} async-done(((f32[768,1536]{1,0:T(8,128)}), f32[48,1536]{1,0:T(8,128)}) %reduce-scatter.30.cloned.1.call-update) | async-done | bytes 294928 | tf_op jit(solution)/shard_map/reduce_scatter | solution.py:143
  824.3 126.4 %reduce-scatter.28.cloned.1.call-done = f32[384,48]{0,1:T(8,128)} async-done(((f32[384,768]{0,1:T(8,128)}), f32[384,48]{0,1:T(8,128)}) %reduce-scatter.28.cloned.1.call-update) | async-done | bytes 73744 | tf_op jit(solution)/shard_map/reduce_scatter | solution.py:142
  952.2 183.0 %all-reduce.7.cloned.1.call-done = f32[3,768,384]{2,0,1:T(4,128)} async-done(((f32[3,768,384]{2,0,1:T(4,128)}), f32[3,768,384]{2,0,1:T(4,128)}) %all-reduce.7.cloned.1.call-update) | async-done | bytes 3538960
  1140.9 39.2 %psum.143 = f32[]{:T(128)} all-reduce(f32[]{:T(128)S(6)} %add.324), channel_id=1, replica_groups=mesh['dp'=16,'mp'=2] {'dp','mp'}, use_global_device_ids=true, to_apply=%region_76.77 | all-reduce | flops 1 | bytes 8 | tf_op jit(solution)/shard_map/psum | solution.py:278
  (438 shorter events, 277.6 us)
Async XLA Ops:
  7.2 53.3 %all-gather.34.cloned.1.call-start = ((), (), s32[]{:S(2)}) async-start(), calls=%async_computation.29 | async-start | bytes 2359296 | tf_op jit(solution)/shard_map/all_gather | solution.py:187
  10.1 76.3 %all-gather.14.cloned.1.call-start = ((), (), s32[]{:S(2)}) async-start(), calls=%async_computation.11 | async-start | bytes 1880064 | tf_op jit(solution)/shard_map/all_gather | solution.py:132
  10.8 143.3 %all-gather.32.cloned.1.call-start = ((), (), s32[]{:S(2)}) async-start(), calls=%async_computation.28 | async-start | bytes 2359296 | tf_op jit(solution)/shard_map/all_gather | solution.py:187
  11.5 215.3 %reduce-scatter.16.cloned.1.call-start = ((), (), s32[]{:S(2)}) async-start(), calls=%async_computation.17 | async-start | bytes 4718592 | tf_op jit(solution)/shard_map/reduce_scatter | solution.py:196
  11.7 78.7 %copy-start.86 = (f32[6]{0:T(128)}, f32[6]{0:T(128)S(1)}, u32[]{:S(2)}) copy-start(f32[6]{0:T(128)S(1)} %convert_element_type.135) | copy-start | bytes 76
  11.8 207.9 %copy-start.70 = (f32[384]{0:T(512)}, f32[384]{0:T(512)S(1)}, u32[]{:S(2)}) copy-start(f32[384]{0:T(512)S(1)} %mul.692) | copy-start | bytes 4612
  153.7 80.1 %reduce-scatter.12.cloned.1.call-start = ((), (), s32[]{:S(2)}) async-start(), calls=%async_computation.12 | async-start | bytes 4718592 | tf_op jit(solution)/shard_map/reduce_scatter | solution.py:196
  223.8 76.7 %all-gather.18.cloned.1.call-start = ((), (), s32[]{:S(2)}) async-start(), calls=%async_computation.14 | async-start | bytes 2506752 | tf_op jit(solution)/shard_map/all_gather | solution.py:134
  225.4 85.8 %all-gather.22.cloned.1.call-start = ((), (), s32[]{:S(2)}) async-start(), calls=%async_computation.18 | async-start | bytes 2359296 | tf_op jit(solution)/shard_map/all_gather | solution.py:204
  242.9 81.5 %all-gather.16.cloned.1.call-start = ((), (), s32[]{:S(2)}) async-start(), calls=%async_computation.13 | async-start | bytes 2359296 | tf_op jit(solution)/shard_map/all_gather | solution.py:204
  243.6 147.6 %all-gather.20.cloned.1.call-start = ((), (), s32[]{:S(2)}) async-start(), calls=%async_computation.15 | async-start | bytes 2506752 | tf_op jit(solution)/shard_map/all_gather | solution.py:135
  244.4 163.6 %reduce-scatter.14.cloned.1.call-start = ((), (), s32[]{:S(2)}) async-start(), calls=%async_computation.16 | async-start | bytes 4718592 | tf_op jit(solution)/shard_map/reduce_scatter | solution.py:208
  398.1 24.3 %reduce-scatter.18.cloned.1.call-start = ((), (), s32[]{:S(2)}) async-start(), calls=%async_computation.19 | async-start | bytes 4718592 | tf_op jit(solution)/shard_map/reduce_scatter | solution.py:208
  405.1 49.0 %all-gather.24.cloned.1.call-start = ((), (), s32[]{:S(2)}) async-start(), calls=%async_computation.20 | async-start | bytes 2359296 | tf_op jit(solution)/shard_map/all_gather | solution.py:222
  443.0 27.3 %all-gather.28.cloned.1.call-start = ((), (), s32[]{:S(2)}) async-start(), calls=%async_computation.24 | async-start | bytes 2359296 | tf_op jit(solution)/shard_map/all_gather | solution.py:222
  443.8 43.2 %reduce-scatter.20.cloned.1.call-start = ((), (), s32[]{:S(2)}) async-start(), calls=%async_computation.21 | async-start | bytes 4718592 | tf_op jit(solution)/shard_map/reduce_scatter | solution.py:236
  454.1 11.8 copy-start.89
  470.2 28.5 %reduce-scatter.24.cloned.1.call-start = ((), (), s32[]{:S(2)}) async-start(), calls=%async_computation.25 | async-start | bytes 4718592 | tf_op jit(solution)/shard_map/reduce_scatter | solution.py:236
  470.3 11.8 copy-start.90
  486.5 46.7 %all-gather.26.cloned.1.call-start = ((), (), s32[]{:S(2)}) async-start(), calls=%async_computation.22 | async-start | bytes 2359296 | tf_op jit(solution)/shard_map/all_gather | solution.py:243
  512.0 28.0 %all-gather.30.cloned.1.call-start = ((), (), s32[]{:S(2)}) async-start(), calls=%async_computation.26 | async-start | bytes 2359296 | tf_op jit(solution)/shard_map/all_gather | solution.py:243
  512.6 261.6 %reduce-scatter.32.cloned.1.call-start = ((), (), s32[]{:S(2)}) async-start(), calls=%async_computation.32 | async-start | bytes 5013504 | tf_op jit(solution)/shard_map/reduce_scatter | solution.py:144
  522.2 300.4 %reduce-scatter.30.cloned.1.call-start = ((), (), s32[]{:S(2)}) async-start(), calls=%async_computation.31 | async-start | bytes 5013504 | tf_op jit(solution)/shard_map/reduce_scatter | solution.py:143
  532.9 417.7 %reduce-scatter.28.cloned.1.call-start = ((), (), s32[]{:S(2)}) async-start(), calls=%async_computation.30 | async-start | bytes 1253376 | tf_op jit(solution)/shard_map/reduce_scatter | solution.py:142
  557.1 67.2 %copy-start.5 = (bf16[1024,6,64]{0,2,1:T(8,128)(2,1)S(1)}, bf16[1024,6,64]{0,2,1:T(8,128)(2,1)}, u32[]{:S(2)}) copy-start(bf16[1024,6,64]{0,2,1:T(8,128)(2,1)} %copy-done.4) | copy-start | bytes 2359300
  557.1 67.2 %copy-start.57 = (s32[1,1,1024]{2,1,0:T(1,128)S(1)}, s32[1,1,1024]{2,1,0:T(1,128)}, u32[]{:S(2)}) copy-start(s32[1,1,1024]{2,1,0:T(1,128)} %copy-done.56) | copy-start | bytes 12292
  557.2 67.2 %copy-start.61 = (f32[2,6,512]{2,1,0:T(8,128)S(1)}, f32[2,6,512]{2,1,0:T(8,128)}, u32[]{:S(2)}) copy-start(f32[2,6,512]{2,1,0:T(8,128)} %copy-done.60) | copy-start | bytes 73732
  557.2 67.2 %copy-start.66 = (s32[2,512]{1,0:T(2,128)S(1)}, s32[2,512]{1,0:T(2,128)}, u32[]{:S(2)}) copy-start(s32[2,512]{1,0:T(2,128)} %copy-done.65) | copy-start | bytes 12292
  572.8 12.0 copy-start.1
  605.0 12.3 %copy-start.1 = (f32[6,512,1024]{2,1,0:T(8,128)S(1)}, f32[6,512,1024]{2,1,0:T(8,128)}, u32[]{:S(2)}) copy-start(f32[6,512,1024]{2,1,0:T(8,128)} %copy-done) | copy-start | bytes 37748740 | tf_op jit(solution)/shard_map/while
  623.3 511.9 %all-reduce.7.cloned.1.call-start = ((), (), s32[]{:S(2)}) async-start(), calls=%async_computation.33 | async-start | bytes 9437184
  638.8 12.1 %copy-start.3 = (f32[6,512,1024]{2,1,0:T(8,128)S(1)}, f32[6,512,1024]{2,1,0:T(8,128)}, u32[]{:S(2)}) copy-start(f32[6,512,1024]{2,1,0:T(8,128)} %copy-done.2) | copy-start | bytes 37748740 | tf_op jit(solution)/shard_map/while
  669.9 12.1 %copy-start.3 = (f32[6,512,1024]{2,1,0:T(8,128)S(1)}, f32[6,512,1024]{2,1,0:T(8,128)}, u32[]{:S(2)}) copy-start(f32[6,512,1024]{2,1,0:T(8,128)} %copy-done.2) | copy-start | bytes 37748740 | tf_op jit(solution)/shard_map/while
  713.0 476.5 %reduce-scatter.22.cloned.1.call-start = ((), (), s32[]{:S(2)}) async-start(), calls=%async_computation.23 | async-start | bytes 4718592 | tf_op jit(solution)/shard_map/reduce_scatter | solution.py:267
  720.0 472.0 %reduce-scatter.26.cloned.1.call-start = ((), (), s32[]{:S(2)}) async-start(), calls=%async_computation.27 | async-start | bytes 4718592 | tf_op jit(solution)/shard_map/reduce_scatter | solution.py:267
  727.0 412.5 %copy-start.30 = (bf16[1,1024,384]{2,1,0:T(8,128)(2,1)S(1)}, bf16[1,1024,384]{2,1,0:T(8,128)(2,1)}, u32[]{:S(2)}) copy-start(bf16[1,1024,384]{2,1,0:T(8,128)(2,1)} %get-tuple-element.679) | copy-start | bytes 2359300
  727.0 412.5 %copy-start.31 = (bf16[1,1024,384]{2,1,0:T(8,128)(2,1)S(1)}, bf16[1,1024,384]{2,1,0:T(8,128)(2,1)}, u32[]{:S(2)}) copy-start(bf16[1,1024,384]{2,1,0:T(8,128)(2,1)} %get-tuple-element.680) | copy-start | bytes 2359300
  728.7 452.2 %copy-start.73 = (f32[4,384]{1,0:T(4,128)S(1)}, f32[4,384]{1,0:T(4,128)}, u32[]{:S(2)}) copy-start(f32[4,384]{1,0:T(4,128)} %param.41) | copy-start | bytes 18436
  728.7 452.2 %copy-start.84 = (f32[4,384]{1,0:T(4,128)S(1)}, f32[4,384]{1,0:T(4,128)}, u32[]{:S(2)}) copy-start(f32[4,384]{1,0:T(4,128)} %param.46) | copy-start | bytes 18436
  728.7 452.2 %copy-start.85 = (f32[4,384]{1,0:T(4,128)S(1)}, f32[4,384]{1,0:T(4,128)}, u32[]{:S(2)}) copy-start(f32[4,384]{1,0:T(4,128)} %param.51) | copy-start | bytes 18436
  728.7 452.8 %copy-start.63 = (f32[384,48]{0,1:T(8,128)S(1)}, f32[384,48]{0,1:T(8,128)}, u32[]{:S(2)}) copy-start(f32[384,48]{0,1:T(8,128)} %param.38) | copy-start | bytes 221188
  728.7 452.8 %copy-start.69 = (f32[384,48]{0,1:T(8,128)S(1)}, f32[384,48]{0,1:T(8,128)}, u32[]{:S(2)}) copy-start(f32[384,48]{0,1:T(8,128)} %param.43) | copy-start | bytes 221188
  775.9 407.2 %copy-start.43 = (f32[3,48,384]{2,1,0:T(8,128)S(1)}, f32[3,48,384]{2,1,0:T(8,128)}, u32[]{:S(2)}) copy-start(f32[3,48,384]{2,1,0:T(8,128)} %param.37) | copy-start | bytes 663556
  950.7 230.8 %copy-start.64 = (f32[384,48]{0,1:T(8,128)S(1)}, f32[384,48]{0,1:T(8,128)}, u32[]{:S(2)}) copy-start(f32[384,48]{0,1:T(8,128)} %reduce-scatter.28.cloned.1.call-done) | copy-start | bytes 221188
  1139.5 45.6 %copy-start.37 = (f32[1536,48]{0,1:T(8,128)S(1)}, f32[1536,48]{0,1:T(8,128)}, u32[]{:S(2)}) copy-start(f32[1536,48]{0,1:T(8,128)} %param.40) | copy-start | bytes 884740
  1139.5 45.5 %copy-start.40 = (f32[1536,48]{0,1:T(8,128)S(1)}, f32[1536,48]{0,1:T(8,128)}, u32[]{:S(2)}) copy-start(f32[1536,48]{0,1:T(8,128)} %reduce-scatter.32.cloned.1.call-done) | copy-start | bytes 884740
  1140.9 46.5 %copy-start.39 = (f32[48,1536]{1,0:T(8,128)S(1)}, f32[48,1536]{1,0:T(8,128)}, u32[]{:S(2)}) copy-start(f32[48,1536]{1,0:T(8,128)} %param.39) | copy-start | bytes 884740
  1140.9 46.5 %copy-start.41 = (f32[48,1536]{1,0:T(8,128)S(1)}, f32[48,1536]{1,0:T(8,128)}, u32[]{:S(2)}) copy-start(f32[48,1536]{1,0:T(8,128)} %reduce-scatter.30.cloned.1.call-done) | copy-start | bytes 884740
  (83 other events, 302.8 us)
Sparse Core Ops, SparseCore 0:
  10.2 12.4 all-gather.33
  25.9 60.3 all-gather.13
  88.5 8.5 all-gather.31
  153.8 9.5 reduce-scatter.15
  224.0 9.8 reduce-scatter.11
  237.1 63.4 all-gather.17
  302.6 8.5 all-gather.21
  313.4 10.9 all-gather.15
  327.7 63.4 all-gather.19
  398.2 9.7 reduce-scatter.13
  410.3 12.0 reduce-scatter.17
  443.1 10.9 all-gather.23
  455.7 10.9 all-gather.27
  470.4 12.0 reduce-scatter.19
  486.6 12.0 reduce-scatter.23
  512.2 11.0 all-gather.25
  524.6 10.9 all-gather.29
  540.6 139.0 reduce-scatter.31
  685.7 136.9 reduce-scatter.29
  827.2 123.3 reduce-scatter.27
  956.4 178.7 all-reduce.6
  1137.5 9.9 reduce-scatter.21
  1149.7 12.0 reduce-scatter.25
where the time goes:
time: 1220 us; the launch traced here: 1200 us
  waiting for transfers between devices  532 us (44%)
  matrix products  271 us (22%)
  blocking collectives  144 us (12%)
  local copies, waits for them, and re-layouts  125 us (10%)
  other arithmetic  105 us (9%)
  between operations  21.3 us (2%)
    unnamed x24, waiting for transfers between devices  186 us
    reduce_scatter x1, waiting for transfers between devices, scatter_grads(): lax.psum_scatter(grad_set[1], 'dp', scatter_dimension=1, tiled=True)  126 us
    dynamic_update_slice x8, local copies, waits for them, and re-layouts, attend_forward(): lax.map(one_block, (queries.reshape(blocks, BLOCK, heads_here, head_width...  63.2 us
    all_gather x1, waiting for transfers between devices, gather_weights(): lax.all_gather(w_in.astype(jnp.bfloat16), 'dp', axis=0, tiled=True)  56.1 us
    all_gather x1, blocking collectives, gather_weights(): lax.all_gather(w_out.astype(jnp.bfloat16), 'dp', axis=1, tiled=True)  48.7 us
    reduce_scatter x1, waiting for transfers between devices, scatter_grads(): lax.psum_scatter(grad_set[2], 'dp', scatter_dimension=0, tiled=True)  46.7 us
    psum x1, blocking collectives, shards(): norm_total = lax.psum(norm_rows, 'dp')  42.8 us
    dot_general x2, matrix products, shards(): pre_act = jnp.dot(normed_full, full_in, preferred_element_type=jnp.float32)  40.1 us
  transfers between devices with their start and end apart: 23, of which 13 were waited for; matrix products, arithmetic and copies ran while one was open for 37% of the time, Pallas kernels for 0%

commit v1 on v0

v1 whole, which is shorter than its diff:
```python
import jax
import jax.numpy as jnp
from jax import lax
from jax.experimental import pallas as pl
from jax.experimental.pallas import tpu as pltpu
from jax.sharding import PartitionSpec as P

D = 768
HEAD_DIM = 64
SEQ = 1024
STEP = 10
TILE = 256
TILES = SEQ // TILE
PAIR = 128

LN_EPS = 1e-12
CLIP_NORM = 1.0
LEARN_RATE = 0.06
NORM_RATE = 0.3
WEIGHT_DECAY = 0.01
BETA_ONE = 0.9
BETA_TWO = 0.999
ADAM_EPS = 1e-08
ATTN_SCALE = HEAD_DIM ** (-0.5)
MASK_STEP = float(2**30)
NT = (((1,), (1,)), ((), ()))
NN = (((1,), (0,)), ((), ()))
TN = (((0,), (0,)), ((), ()))
BF = jnp.bfloat16
F32 = jnp.float32


def dot(left, right, dims):
    return lax.dot_general(left, right, dims, preferred_element_type=F32)


def segment_tables(segment):
    first = segment[::TILE]
    last = segment[TILE - 1 :: TILE]
    low = jnp.sum((last[None, :] < first[:, None]).astype(jnp.int32), axis=1)
    high = jnp.sum((first[None, :] <= last[:, None]).astype(jnp.int32), axis=1)
    lane = lax.broadcasted_iota(jnp.int32, (SEQ, PAIR), 1) % HEAD_DIM
    same = lane == segment[:, None]
    key_lanes = jnp.where(same, 1.0, 0.0).astype(BF)
    query_lanes = jnp.where((lane < 4) & (~same), -MASK_STEP, 0.0).astype(BF)
    return low, high, key_lanes, query_lanes


def attend_fwd_kernel(low_ref, high_ref, qkv_ref, klane_ref, qlane_ref, ctx_ref, lse_ref, kh_ref, qh_ref, ls_ref):
    lane = lax.broadcasted_iota(jnp.int32, (SEQ, PAIR), 1)
    query = qkv_ref[:, 0:PAIR] * ATTN_SCALE
    keys = qkv_ref[:, PAIR : 2 * PAIR]
    for h in range(2):
        mine = (lane // HEAD_DIM) == h
        kh_ref[h] = jnp.where(mine, keys, klane_ref[...])
        qh_ref[h] = jnp.where(mine, query, qlane_ref[...])
    is_first = lax.broadcasted_iota(jnp.int32, (TILE, PAIR), 1) < HEAD_DIM

    def row_block(qb, carry):
        low = low_ref[qb]
        count = high_ref[qb] - low
        rows = pl.ds(pl.multiple_of(qb * TILE, TILE), TILE)
        for width in range(1, TILES + 1):

            @pl.when(count == width)
            def _():
                span = pl.ds(pl.multiple_of(low * TILE, TILE), width * TILE)
                scores = [dot(qh_ref[h, rows, :], kh_ref[h, span, :], NT) for h in range(2)]
                tops = [jnp.max(s, axis=1, keepdims=True) for s in scores]
                expo = [jnp.exp(s - m) for s, m in zip(scores, tops)]
                sums = [jnp.sum(p, axis=1, keepdims=True) for p in expo]
                outs = [dot(p.astype(BF), qkv_ref[span, 2 * PAIR : 3 * PAIR], NN) for p in expo]
                ctx_ref[rows, :] = jnp.where(is_first, outs[0] / sums[0], outs[1] / sums[1]).astype(BF)
                ls_ref[rows, :] = jnp.where(
                    is_first, tops[0] + jnp.log(sums[0]), tops[1] + jnp.log(sums[1])
                )

        return carry

    lax.fori_loop(0, TILES, row_block, 0)
    turned = ls_ref[...].T
    lse_ref[0, 0:1, :] = turned[0:1]
    lse_ref[0, 1:2, :] = turned[HEAD_DIM : HEAD_DIM + 1]


def attend_forward(qkv, tables):
    pairs = qkv.shape[1] // (3 * PAIR)
    low, high, key_lanes, query_lanes = tables
    whole = pl.BlockSpec((SEQ, PAIR), lambda p, *_: (0, 0))
    return pl.pallas_call(
        attend_fwd_kernel,
        grid_spec=pltpu.PrefetchScalarGridSpec(
            num_scalar_prefetch=2,
            grid=(pairs,),
            in_specs=[pl.BlockSpec((SEQ, 3 * PAIR), lambda p, *_: (0, p)), whole, whole],
            out_specs=[
                pl.BlockSpec((SEQ, PAIR), lambda p, *_: (0, p)),
                pl.BlockSpec((1, 2, SEQ), lambda p, *_: (p, 0, 0)),
            ],
            scratch_shapes=[
                pltpu.VMEM((2, SEQ, PAIR), BF),
                pltpu.VMEM((2, SEQ, PAIR), BF),
                pltpu.VMEM((SEQ, PAIR), F32),
            ],
        ),
        out_shape=[
            jax.ShapeDtypeStruct((SEQ, pairs * PAIR), BF),
            jax.ShapeDtypeStruct((pairs, 2, SEQ), F32),
        ],
        compiler_params=pltpu.CompilerParams(vmem_limit_bytes=32 << 20),
        cost_estimate=pl.CostEstimate(
            flops=pairs * 4 * SEQ * SEQ * 256, bytes_accessed=pairs * SEQ * 1100, transcendentals=0
        ),
        name="attend_fwd",
    )(low, high, qkv, key_lanes, query_lanes)


def attend_bwd_kernel(
    low_ref, high_ref, qkv_ref, dctx_ref, ctx_ref, lse_ref, klane_ref, qlane_ref, dqkv_ref,
    kh_ref, qh_ref, kt_ref, q0_ref, d0_ref, delta_ref, dqt_ref,
):
    lane = lax.broadcasted_iota(jnp.int32, (SEQ, PAIR), 1)
    query = qkv_ref[:, 0:PAIR] * ATTN_SCALE
    keys = qkv_ref[:, PAIR : 2 * PAIR]
    dctx = dctx_ref[...]
    kt_ref[...] = keys.T
    prod = (dctx.astype(F32) * ctx_ref[...].astype(F32)).T
    zero = jnp.zeros((SEQ, PAIR), BF)
    for h in range(2):
        mine = (lane // HEAD_DIM) == h
        kh_ref[h] = jnp.where(mine, keys, klane_ref[...])
        qh_ref[h] = jnp.where(mine, query, qlane_ref[...])
        q0_ref[h] = jnp.where(mine, query, zero)
        d0_ref[h] = jnp.where(mine, dctx, zero)
        delta_ref[h : h + 1, :] = jnp.sum(
            prod[h * HEAD_DIM : (h + 1) * HEAD_DIM], axis=0, keepdims=True
        )
    dqt_ref[...] = jnp.zeros((PAIR, SEQ), F32)

    def key_block(kb, carry):
        low = low_ref[kb]
        count = high_ref[kb] - low
        cols = pl.ds(pl.multiple_of(kb * TILE, TILE), TILE)
        for width in range(1, TILES + 1):

            @pl.when(count == width)
            def _():
                span = pl.ds(pl.multiple_of(low * TILE, TILE), width * TILE)
                values = qkv_ref[cols, 2 * PAIR : 3 * PAIR]
                scores = [dot(kh_ref[h, cols, :], qh_ref[h, span, :], NT) for h in range(2)]
                dprob = [dot(values, d0_ref[h, span, :], NT) for h in range(2)]
                prob = [jnp.exp(scores[h] - lse_ref[0, h : h + 1, span]) for h in range(2)]
                low_p = [p.astype(BF) for p in prob]
                dscore = [
                    (prob[h] * (dprob[h] - delta_ref[h : h + 1, span])).astype(BF) for h in range(2)
                ]
                dvals = dot(low_p[0], d0_ref[0, span, :], NN) + dot(low_p[1], d0_ref[1, span, :], NN)
                dkeys = dot(dscore[0], q0_ref[0, span, :], NN) + dot(dscore[1], q0_ref[1, span, :], NN)
                for h in range(2):
                    part = slice(h * HEAD_DIM, (h + 1) * HEAD_DIM)
                    dqt_ref[part, span] += dot(kt_ref[part, cols], dscore[h], NN)
                dqkv_ref[cols, PAIR : 2 * PAIR] = dkeys.astype(BF)
                dqkv_ref[cols, 2 * PAIR : 3 * PAIR] = dvals.astype(BF)

        return carry

    lax.fori_loop(0, TILES, key_block, 0)
    dqkv_ref[:, 0:PAIR] = (dqt_ref[...].T * ATTN_SCALE).astype(BF)


def attend_backward(qkv, dctx, ctx, lse, tables):
    pairs = qkv.shape[1] // (3 * PAIR)
    low, high, key_lanes, query_lanes = tables
    whole = pl.BlockSpec((SEQ, PAIR), lambda p, *_: (0, 0))
    column = pl.BlockSpec((SEQ, PAIR), lambda p, *_: (0, p))
    triple = pl.BlockSpec((SEQ, 3 * PAIR), lambda p, *_: (0, p))
    return pl.pallas_call(
        attend_bwd_kernel,
        grid_spec=pltpu.PrefetchScalarGridSpec(
            num_scalar_prefetch=2,
            grid=(pairs,),
            in_specs=[
                triple, column, column, pl.BlockSpec((1, 2, SEQ), lambda p, *_: (p, 0, 0)), whole, whole,
            ],
            out_specs=triple,
            scratch_shapes=[
                pltpu.VMEM((2, SEQ, PAIR), BF),
                pltpu.VMEM((2, SEQ, PAIR), BF),
                pltpu.VMEM((PAIR, SEQ), BF),
                pltpu.VMEM((2, SEQ, PAIR), BF),
                pltpu.VMEM((2, SEQ, PAIR), BF),
                pltpu.VMEM((2, SEQ), F32),
                pltpu.VMEM((PAIR, SEQ), F32),
            ],
        ),
        out_shape=jax.ShapeDtypeStruct((SEQ, pairs * 3 * PAIR), BF),
        compiler_params=pltpu.CompilerParams(vmem_limit_bytes=32 << 20),
        cost_estimate=pl.CostEstimate(
            flops=pairs * 8 * SEQ * SEQ * 256, bytes_accessed=pairs * SEQ * 2100, transcendentals=0
        ),
        name="attend_bwd",
    )(low, high, qkv, dctx, ctx, lse, key_lanes, query_lanes)


def gelu_pair(value):
    size = jnp.abs(value)
    bell = jnp.exp(-0.5 * value * value)
    step = 1.0 / (1.0 + (0.3275911 * 0.7071067811865476) * size)
    poly = step * (
        0.127414796
        + step * (-0.142248368 + step * (0.7107068705 + step * (-0.7265760135 + step * 0.5307027145)))
    )
    tail = poly * bell
    phi = jnp.where(value >= 0.0, 1.0 - tail, tail)
    return value * phi, phi + value * bell * 0.3989422804014327


def ffn_in_kernel(x_ref, w_ref, act_ref, slope_ref):
    pre = dot(x_ref[...], w_ref[...], NN)
    act, slope = gelu_pair(pre)
    act_ref[...] = act.astype(BF)
    slope_ref[...] = slope.astype(BF)


def ffn_in(normed, weight):
    units = weight.shape[1]
    width = 256
    return pl.pallas_call(
        ffn_in_kernel,
        grid=(units // width,),
        in_specs=[
            pl.BlockSpec((SEQ, D), lambda n: (0, 0)),
            pl.BlockSpec((D, width), lambda n: (0, n)),
        ],
        out_specs=[pl.BlockSpec((SEQ, width), lambda n: (0, n))] * 2,
        out_shape=[jax.ShapeDtypeStruct((SEQ, units), BF)] * 2,
        compiler_params=pltpu.CompilerParams(vmem_limit_bytes=32 << 20),
        cost_estimate=pl.CostEstimate(
            flops=4 * SEQ * D * units, bytes_accessed=SEQ * units * 4, transcendentals=0
        ),
        name="ffn_in",
    )(normed, weight)


def digits_of(count):
    found, shift = [], 0
    while (1 << shift) < count:
        radix = min(4, count >> shift)
        found.append((shift, radix))
        shift += 2 if radix == 4 else 1
    return found


def swap(value, count, mask, axis="dp"):
    return lax.ppermute(value, axis, [(i, i ^ mask) for i in range(count)])


def place_kernel(digit_ref, *refs):
    pieces, out, sems = refs[:-2], refs[-2], refs[-1]
    digit = digit_ref[0]
    copies = [
        pltpu.make_async_copy(piece, out.at[:, digit ^ j], sems.at[j]) for j, piece in enumerate(pieces)
    ]
    for copy in copies:
        copy.start()
    for copy in copies:
        copy.wait()


def place(pieces, digit):
    outer, rows, cols = pieces[0].shape
    radix = len(pieces)
    return pl.pallas_call(
        place_kernel,
        grid_spec=pltpu.PrefetchScalarGridSpec(
            num_scalar_prefetch=1,
            grid=(),
            in_specs=[pl.BlockSpec(memory_space=pl.ANY)] * radix,
            out_specs=pl.BlockSpec(memory_space=pl.ANY),
            scratch_shapes=[pltpu.SemaphoreType.DMA((radix,))],
        ),
        out_shape=jax.ShapeDtypeStruct((outer, radix, rows, cols), pieces[0].dtype),
        cost_estimate=pl.CostEstimate(
            flops=0, bytes_accessed=outer * radix * rows * cols * 4, transcendentals=0
        ),
        name="place",
    )(digit[None], *pieces)


def gather_rows(shard, count, index):
    rows, cols = shard.shape
    held = shard[None]
    for shift, radix in reversed(digits_of(count)):
        pieces = [held] + [swap(held, count, j << shift) for j in range(1, radix)]
        held = place(pieces, (index >> shift) & (radix - 1)).reshape(-1, rows, cols)
    return held.reshape(-1, cols)


def scatter_rows(total, count, index):
    rows, cols = total.shape[0] // count, total.shape[1]
    held = total
    for shift, radix in digits_of(count):
        digit = (index >> shift) & (radix - 1)
        parts = held.reshape(-1, radix, rows, cols)
        own = lax.dynamic_index_in_dim(parts, digit, 1, keepdims=False).astype(F32)
        for j in range(1, radix):
            away = lax.dynamic_index_in_dim(parts, digit ^ j, 1, keepdims=False)
            own = own + swap(away.astype(BF), count, j << shift).astype(F32)
        held = own
        if shift != digits_of(count)[-1][0]:
            held = held.astype(BF)
    return held.reshape(rows, cols)


def sum_all(value, count):
    value = value + swap(value, 2, 1, "mp")
    for shift, radix in digits_of(count):
        parts = [value] + [swap(value, count, j << shift) for j in range(1, radix)]
        value = parts[0] + parts[1]
        if radix == 4:
            value = value + (parts[2] + parts[3])
    return value


def norm_forward(residual, gain_vec, shift_vec):
    mean_val = jnp.sum(residual, axis=-1, keepdims=True) / D
    var_val = jnp.sum(residual * residual, axis=-1, keepdims=True) / D - mean_val * mean_val
    inv_std = lax.rsqrt(var_val + LN_EPS)
    centred = (residual - mean_val) * inv_std
    return (centred * gain_vec + shift_vec, centred, inv_std)


def norm_backward(grad_out, centred, inv_std, gain_vec):
    scaled = grad_out * gain_vec
    mean_one = jnp.sum(scaled, axis=-1, keepdims=True) / D
    mean_two = jnp.sum(scaled * centred, axis=-1, keepdims=True) / D
    grad_in = inv_std * (scaled - mean_one - centred * mean_two)
    return (grad_in, jnp.sum(grad_out * centred, axis=0), jnp.sum(grad_out, axis=0))


def adam_step(weight, gradient, first_mom, second, step_rate, decay_rate):
    first_new = BETA_ONE * first_mom + (1.0 - BETA_ONE) * gradient
    second_new = BETA_TWO * second + (1.0 - BETA_TWO) * gradient * gradient
    update = (
        first_new
        / (1.0 - BETA_ONE**STEP)
        / (jnp.sqrt(second_new / (1.0 - BETA_TWO**STEP)) + ADAM_EPS)
    )
    return (weight - step_rate * (update + decay_rate * weight), first_new, second_new)


def shards(
    count,
    tokens,
    cotangent,
    segments,
    head_gates,
    unit_gates,
    hidden_gates,
    layer_gates,
    w_qkv,
    w_out,
    w_in,
    w_back,
    norm_params,
    mom_qkv,
    mom_out,
    mom_in,
    mom_back,
    mom_norm,
    sec_qkv,
    sec_out,
    sec_in,
    sec_back,
    sec_norm,
):
    index = lax.axis_index("dp")
    core = lax.axis_index("mp")
    rows = D // count
    half = D // 2
    pairs = half // PAIR
    head_mask = jnp.repeat(head_gates.astype(F32), HEAD_DIM)
    unit_mask = unit_gates.astype(F32)
    gate_attn = layer_gates[0]
    gate_ffn = layer_gates[1]

    shard_qkv = (
        w_qkv.astype(BF).reshape(3, rows, pairs, PAIR).transpose(1, 2, 0, 3).reshape(rows, 3 * half)
    )
    shard_out = (w_out.T * head_mask[None, :]).astype(BF)
    shard_one = jnp.concatenate([shard_qkv, shard_out], axis=1)
    shard_in = w_in.astype(BF)
    shard_back = (w_back.T * unit_mask[None, :]).astype(BF)

    def other_core(value):
        return swap(value, 2, 1, "mp")

    def both(own, away):
        return jnp.where(
            core == 0, jnp.concatenate([own, away], axis=-1), jnp.concatenate([away, own], axis=-1)
        )

    mine_one = gather_rows(shard_one, count, index)
    away_one = other_core(mine_one)
    mine_in = gather_rows(shard_in, count, index)
    away_in = other_core(mine_in)
    mine_back = gather_rows(shard_back, count, index)
    away_back = other_core(mine_back)
    qkv_sides = (mine_one[:, : 3 * half], away_one[:, : 3 * half])
    out_sides = (mine_one[:, 3 * half :], away_one[:, 3 * half :])
    in_sides = (mine_in, away_in)
    back_sides = (mine_back, away_back)

    def bring(value):
        own = lax.dynamic_index_in_dim(value, core, 0, keepdims=False)
        away = other_core(lax.dynamic_index_in_dim(value, 1 - core, 0, keepdims=False))
        return both(own, away)

    x = bring(tokens)
    grad_out = bring(cotangent)
    vectors = jnp.concatenate([hidden_gates.astype(F32)[None], norm_params], axis=0)
    vectors = both(vectors, other_core(vectors))
    hidden_mask, params = vectors[0], vectors[1:]
    segment = lax.dynamic_index_in_dim(segments, core, 0, keepdims=False)[0]
    tables = segment_tables(segment)

    qkv = [dot(x, side, NN).astype(BF) for side in qkv_sides]
    ctx, lse = [], []
    for side in range(2):
        context, log_sum = attend_forward(qkv[side], tables)
        ctx.append(context)
        lse.append(log_sum)
    attn = dot(ctx[0], out_sides[0], NT) + dot(ctx[1], out_sides[1], NT)
    resid_one = x.astype(F32) + (gate_attn * hidden_mask) * attn
    normed, centred_one, inv_one = norm_forward(resid_one, params[0], params[1])
    normed_low = normed.astype(BF)
    acts, slopes = [], []
    for side in range(2):
        act, slope = ffn_in(normed_low, in_sides[side])
        acts.append(act)
        slopes.append(slope)
    ffn = dot(acts[0], back_sides[0], NT) + dot(acts[1], back_sides[1], NT)
    resid_two = normed + (gate_ffn * hidden_mask) * ffn
    result, centred_two, inv_two = norm_forward(resid_two, params[2], params[3])

    grad_two, dgain_two, dshift_two = norm_backward(
        grad_out.astype(F32), centred_two, inv_two, params[2]
    )
    grad_ffn = ((gate_ffn * hidden_mask) * grad_two).astype(BF)

    def reduce_group(own, away):
        summed = own.astype(F32) + other_core(away.astype(BF)).astype(F32)
        return scatter_rows(summed.astype(BF), count, index)

    g_back = [dot(grad_ffn, act, TN).astype(BF) for act in acts]
    sum_back = reduce_group(*g_back)
    grad_pre = [
        (dot(grad_ffn, back_sides[s], NN) * slopes[s].astype(F32)).astype(BF) for s in range(2)
    ]
    g_in = [dot(normed_low, g, TN).astype(BF) for g in grad_pre]
    sum_in = reduce_group(*g_in)
    grad_normed = grad_two + (dot(grad_pre[0], in_sides[0], NT) + dot(grad_pre[1], in_sides[1], NT))
    grad_one, dgain_one, dshift_one = norm_backward(grad_normed, centred_one, inv_one, params[0])
    grad_attn = ((gate_attn * hidden_mask) * grad_one).astype(BF)
    g_out = [dot(grad_attn, context, TN).astype(BF) for context in ctx]
    dqkv = []
    for side in range(2):
        dctx = dot(grad_attn, out_sides[side], NN).astype(BF)
        dqkv.append(attend_backward(qkv[side], dctx, ctx[side], lse[side], tables))
    g_qkv = [dot(x, g, TN).astype(BF) for g in dqkv]
    sum_one = reduce_group(*[jnp.concatenate(pair, axis=1) for pair in zip(g_qkv, g_out)])
    grad_tok = grad_one + (dot(dqkv[0], qkv_sides[0], NT) + dot(dqkv[1], qkv_sides[1], NT))

    def send_back(value):
        first, second = value[:, :half], value[:, half:]
        own = jnp.where(core == 0, first, second)
        away = other_core(jnp.where(core == 0, second, first))
        return jnp.where(core == 0, jnp.stack([own, away]), jnp.stack([away, own]))

    out_tokens = send_back(result.astype(BF))
    input_grad = send_back(grad_tok.astype(BF))

    sum_qkv = sum_one[:, : 3 * half].reshape(rows, pairs, 3, PAIR).transpose(2, 0, 1, 3)
    sum_qkv = sum_qkv.reshape(3, rows, half)
    sum_out = (sum_one[:, 3 * half :] * head_mask[None, :]).T
    sum_wb = (sum_back * unit_mask[None, :]).T
    sums = (sum_qkv, sum_out, sum_in, sum_wb)
    square = sum(jnp.sum(g * g) for g in sums)
    norm_rows = jnp.stack([dgain_one, dshift_one, dgain_two, dshift_two]).reshape(-1, 128)
    packed = jnp.concatenate([norm_rows, jnp.full((8, 128), square / 1024.0, F32)], axis=0)
    packed = sum_all(packed, count)
    norm_full = packed[:-8].reshape(4, D)
    total_square = jnp.sum(packed[-8:]) + jnp.sum(norm_full * norm_full)
    grad_norm = jnp.sqrt(total_square)
    factor = jnp.minimum(1.0, CLIP_NORM / grad_norm)
    norm_here = lax.dynamic_slice_in_dim(norm_full, core * half, half, 1)
    weights = (w_qkv, w_out, w_in, w_back, norm_params)
    firsts = (mom_qkv, mom_out, mom_in, mom_back, mom_norm)
    seconds = (sec_qkv, sec_out, sec_in, sec_back, sec_norm)
    results = []
    for slot, gradient in enumerate(sums + (norm_here,)):
        results.append(
            adam_step(
                weights[slot],
                gradient * factor,
                firsts[slot],
                seconds[slot],
                LEARN_RATE if slot < 4 else NORM_RATE,
                WEIGHT_DECAY if slot < 4 else 0.0,
            )
        )
    return (
        out_tokens,
        input_grad,
        grad_norm,
        *[r[0] for r in results],
        *[r[1] for r in results],
        *[r[2] for r in results],
    )


def solution(mesh):
    weight_specs = (P(None, "dp", "mp"), P("mp", "dp"), P("dp", "mp"), P("mp", "dp"), P(None, "mp"))
    in_specs = (
        P(None, "dp", "mp"),
        P(None, "dp", "mp"),
        P(None, "dp", None),
        P("mp"),
        P("mp"),
        P("mp"),
        P(),
    ) + weight_specs * 3
    out_specs = (P(None, "dp", "mp"), P(None, "dp", "mp"), P()) + weight_specs * 3
    count = mesh.shape["dp"]

    def body(*args):
        return shards(count, *args)

    return jax.shard_map(body, mesh=mesh, in_specs=in_specs, out_specs=out_specs, check_vma=False)
```

time: 1220 us -> 691 us (0.57)
  waiting for transfers between devices: 532 us -> 115 us
  Pallas kernels: 0 us -> 339 us
  matrix products: 271 us -> 83.2 us
  blocking collectives: 144 us -> 0 us
  local copies, waits for them, and re-layouts: 125 us -> 13.3 us
  starting transfers between devices: 2.25 us -> 83.1 us
  other arithmetic: 105 us -> 43.6 us
  between operations: 21.3 us -> 7.27 us
    pallas_call x0 -> x12, Pallas kernels: none -> 339 us  [the longest x6 275 us: place(): pl.pallas_call(place_kernel, grid_spec=pltpu.PrefetchScalarGridSpec(num_s...]
    reduce_scatter x11 -> x0, waiting for transfers between devices: 203 us -> none  [the longest x1 126 us: scatter_grads(): lax.psum_scatter(grad_set[1], 'dp', scatter_dimension=1, tiled=True)]
    dot_general x52 -> x22, matrix products: 271 us -> 83.2 us  [dot(): return lax.dot_general(left, right, dims, preferred_element_type=F32)]
    unnamed x24 -> x0, waiting for transfers between devices: 186 us -> none
    all_gather x11 -> x0, waiting for transfers between devices: 143 us -> none  [the longest x1 56.1 us: gather_weights(): lax.all_gather(w_in.astype(jnp.bfloat16), 'dp', axis=0, tiled=True)]
    ppermute x0 -> x54, waiting for transfers between devices: none -> 115 us  [swap(): return lax.ppermute(value, axis, [(i, i ^ mask) for i in range(count)])]
    psum x6 -> x0, blocking collectives: 95.7 us -> none  [the longest x1 42.8 us: shards(): norm_total = lax.psum(norm_rows, 'dp')]
    ppermute x0 -> x54, starting transfers between devices: none -> 83.1 us  [swap(): return lax.ppermute(value, axis, [(i, i ^ mask) for i in range(count)])]
  transfers between devices with their start and end apart: 23 -> 54, of which waited for: 13 -> 18; matrix products, arithmetic and copies ran while one was open for 37% -> 12% of each run, Pallas kernels for 0% -> 47%
where the time goes in v1:
time: 691 us; the launch traced here: 685 us
  Pallas kernels  339 us (49%)
  waiting for transfers between devices  115 us (17%)
  matrix products  83.2 us (12%)
  starting transfers between devices  83.1 us (12%)
  other arithmetic  43.6 us (6%)
  local copies, waits for them, and re-layouts  13.3 us (2%)
  between operations  7.27 us (1%)
    pallas_call x6, Pallas kernels, place(): pl.pallas_call(place_kernel, grid_spec=pltpu.PrefetchScalarGridSpec(num_s...  275 us
    ppermute x54, waiting for transfers between devices, swap(): return lax.ppermute(value, axis, [(i, i ^ mask) for i in range(count)])  115 us
    dot_general x22, matrix products, dot(): return lax.dot_general(left, right, dims, preferred_element_type=F32)  83.2 us
    ppermute x54, starting transfers between devices, swap(): return lax.ppermute(value, axis, [(i, i ^ mask) for i in range(count)])  83.1 us
    pallas_call x2, Pallas kernels, attend_backward(): pl.pallas_call(attend_bwd_kernel, grid_spec=pltpu.PrefetchScalarGridSpec(...  27.5 us
    pallas_call x2, Pallas kernels, attend_forward(): pl.pallas_call(attend_fwd_kernel, grid_spec=pltpu.PrefetchScalarGridSpec(...  19.4 us
    pallas_call x2, Pallas kernels, ffn_in(): pl.pallas_call(ffn_in_kernel, grid=(units // width,), in_specs=[pl.BlockS...  17.7 us
  transfers between devices with their start and end apart: 54, of which 18 were waited for; matrix products, arithmetic and copies ran while one was open for 12% of the time, Pallas kernels for 47%

profile of v1, /device:TPU:0, one launch (start us, length us, event | category | flops | bytes accessed | tf_op | source)
XLA Modules:
  0.0 684.9 jit_solution(12516436983085032534)
XLA Ops:
  12.7 8.1 %collective-permute-done.3.refs_2_ = bf16[1,48,1536]{2,1,0:T(8,128)(2,1)S(1)} collective-permute-done((bf16[1,48,1536]{2,1,0:T(8,128)(2,1)S(1)}, bf16[1,48,1536]{2,1,0:T(8,128)(2,1)S(1)}, u32[]{:S(2)}, u32[]{:S(2)}) %collective-permute-start.3) | collective-permute-done | bytes 147488 | tf_op jit(solution)/shard_map/ppermute | solution.py:255
  21.5 19.0 %place.6 = bf16[1,4,48,1536]{3,2,1,0:T(8,128)(2,1)} custom-call(s32[1]{0:T(128)} %bitcast.5.digit_ref, bf16[1,48,1536]{2,1,0:T(8,128)(2,1)} %copy-done.34, bf16[1,48,1536]{2,1,0:T(8,128)(2,1)} %copy-done.42, bf16[1,48,1536]{2,1,0:T(8,128)(2,1)} %copy-done.44, bf16[1,48,1536]{2,1,0:T(8,128)(2,1)} %copy-done.45), custom_call_target="tpu_custom_call" | custom-call | bytes 1179648 | tf_op jit(solution)/shard_map/place/pallas_call | solution.py:273
  49.4 7.6 %collective-permute-done.5.refs_1_ = bf16[4,48,1536]{2,1,0:T(8,128)(2,1)S(1)} collective-permute-done((bf16[4,48,1536]{2,1,0:T(8,128)(2,1)}, bf16[4,48,1536]{2,1,0:T(8,128)(2,1)S(1)}, u32[]{:S(2)}, u32[]{:S(2)}) %collective-permute-start.5) | collective-permute-done | bytes 589856 | tf_op jit(solution)/shard_map/ppermute | solution.py:255
  59.3 7.9 %collective-permute-done.6.refs_2_ = bf16[4,48,1536]{2,1,0:T(8,128)(2,1)S(1)} collective-permute-done((bf16[4,48,1536]{2,1,0:T(8,128)(2,1)}, bf16[4,48,1536]{2,1,0:T(8,128)(2,1)S(1)}, u32[]{:S(2)}, u32[]{:S(2)}) %collective-permute-start.6) | collective-permute-done | bytes 589856 | tf_op jit(solution)/shard_map/ppermute | solution.py:255
  68.3 72.6 %place.7 = bf16[4,4,48,1536]{3,2,1,0:T(8,128)(2,1)} custom-call(s32[1]{0:T(128)} %bitcast.4.digit_ref, bf16[4,48,1536]{2,1,0:T(8,128)(2,1)} %bitcast.149, bf16[4,48,1536]{2,1,0:T(8,128)(2,1)} %copy-done.30, bf16[4,48,1536]{2,1,0:T(8,128)(2,1)} %copy-done.31, bf16[4,48,1536]{2,1,0:T(8,128)(2,1)} %copy-done.32), custom_call_target="tpu_custom_call" | custom-call | bytes 4718592 | tf_op jit(solution)/shard_map/place/pallas_call | solution.py:273
  142.0 3.6 collective-permute-start.15
  145.6 19.0 %place.8 = bf16[1,4,48,1536]{3,2,1,0:T(8,128)(2,1)} custom-call(s32[1]{0:T(128)} %bitcast.5.digit_ref, bf16[1,48,1536]{2,1,0:T(8,128)(2,1)} %convert_bitcast_fusion.refs_0_, bf16[1,48,1536]{2,1,0:T(8,128)(2,1)} %collective-permute-done.9.refs_1_, bf16[1,48,1536]{2,1,0:T(8,128)(2,1)} %collective-permute-done.10.refs_2_, ...), custom_call_target="tpu_custom_call" | custom-call | bytes 1179648 | tf_op jit(solution)/shard_map/place/pallas_call | solution.py:273
  171.3 6.6 collective-permute-done.16.refs_2_
  181.6 3.9 collective-permute-done.17.refs_3_
  186.2 19.0 %place.10 = bf16[1,4,48,1536]{3,2,1,0:T(8,128)(2,1)} custom-call(s32[1]{0:T(128)} %bitcast.5.digit_ref, bf16[1,48,1536]{2,1,0:T(8,128)(2,1)} %fusion.36.refs_0_, bf16[1,48,1536]{2,1,0:T(8,128)(2,1)} %copy-done.40, bf16[1,48,1536]{2,1,0:T(8,128)(2,1)} %copy-done.43, bf16[1,48,1536]{2,1,0:T(8,128)(2,1)} %copy-done.46), custom_call_target="tpu_custom_call" | custom-call | bytes 1179648 | tf_op jit(solution)/shard_map/place/pallas_call | solution.py:273
  210.8 72.6 %place.9 = bf16[4,4,48,1536]{3,2,1,0:T(8,128)(2,1)} custom-call(s32[1]{0:T(128)} %bitcast.4.digit_ref, bf16[4,48,1536]{2,1,0:T(8,128)(2,1)} %bitcast.141, bf16[4,48,1536]{2,1,0:T(8,128)(2,1)} %collective-permute-done.12.refs_1_, bf16[4,48,1536]{2,1,0:T(8,128)(2,1)} %collective-permute-done.13.refs_2_, bf16[4,48,1536]{2,1,0:T(8,128)(2,1)} %collective-permute-done.14.refs_3_), custom_call_target="tpu_custom_call" | custom-call | bytes 4718592 | tf_op jit(solution)/shard_map/place/pallas_call | solution.py:273
  284.8 72.6 %place.11 = bf16[4,4,48,1536]{3,2,1,0:T(8,128)(2,1)} custom-call(s32[1]{0:T(128)} %bitcast.4.digit_ref, bf16[4,48,1536]{2,1,0:T(8,128)(2,1)} %bitcast.145, bf16[4,48,1536]{2,1,0:T(8,128)(2,1)} %copy-done.28, bf16[4,48,1536]{2,1,0:T(8,128)(2,1)} %copy-done.29, bf16[4,48,1536]{2,1,0:T(8,128)(2,1)} %collective-permute-done.20.refs_3_), custom_call_target="tpu_custom_call" | custom-call | bytes 4718592 | tf_op jit(solution)/shard_map/place/pallas_call | solution.py:273
  357.6 4.1 convolution_convert_fusion.1.qkv_ref
  361.7 9.8 %attend_fwd.2 = (bf16[1024,384]{1,0:T(8,128)(2,1)S(1)}, f32[3,2,1024]{2,1,0:T(2,128)S(1)}) custom-call(s32[4]{0:T(128)S(1)} %get-tuple-element.52.low_ref, s32[4]{0:T(128)S(1)} %get-tuple-element.51.high_ref, bf16[1024,1152]{1,0:T(8,128)(2,1)S(1)} %convolution_convert_fusion.1.qkv_ref, bf16[1024,128]{1,0:T(8,128)(2,1)S(1)} %get-tuple-element.106.klane_ref, ...), custom_call_target="tpu_custom_call" | custom-call | flops 3221225472 | bytes 3379200 | tf_op jit(solution)/shard_map/attend_fwd/pallas_call | solution.py:90
  371.6 4.2 convolution_convert_fusion.qkv_ref
  375.8 9.6 %attend_fwd.3 = (bf16[1024,384]{1,0:T(8,128)(2,1)S(1)}, f32[3,2,1024]{2,1,0:T(2,128)S(1)}) custom-call(s32[4]{0:T(128)S(1)} %get-tuple-element.52.low_ref, s32[4]{0:T(128)S(1)} %get-tuple-element.51.high_ref, bf16[1024,1152]{1,0:T(8,128)(2,1)S(1)} %convolution_convert_fusion.qkv_ref, bf16[1024,128]{1,0:T(8,128)(2,1)S(1)} %get-tuple-element.106.klane_ref, ...), custom_call_target="tpu_custom_call" | custom-call | flops 3221225472 | bytes 3379200 | tf_op jit(solution)/shard_map/attend_fwd/pallas_call | solution.py:90
  392.4 8.1 %ffn_in.2 = (bf16[1024,1536]{1,0:T(8,128)(2,1)S(1)}, bf16[1024,1536]{1,0:T(8,128)(2,1)S(1)}) custom-call(bf16[1024,768]{1,0:T(8,128)(2,1)S(1)} %fusion.7.x_ref, bf16[768,1536]{1,0:T(8,128)(2,1)S(1)} %bitcast.132), custom_call_target="tpu_custom_call" | custom-call | flops 4831838208 | bytes 6291456 | tf_op jit(solution)/shard_map/ffn_in/pallas_call | solution.py:228
  400.4 9.6 %ffn_in.3 = (bf16[1024,1536]{1,0:T(8,128)(2,1)S(1)}, bf16[1024,1536]{1,0:T(8,128)(2,1)S(1)}) custom-call(bf16[1024,768]{1,0:T(8,128)(2,1)S(1)} %fusion.7.x_ref, bf16[768,1536]{1,0:T(8,128)(2,1)} %collective-permute-done.21.w_ref), custom_call_target="tpu_custom_call" | custom-call | flops 4831838208 | bytes 6291456 | tf_op jit(solution)/shard_map/ffn_in/pallas_call | solution.py:228
  410.1 6.0 fusion.54
  416.1 5.9 fusion.42
  425.7 4.4 multiply_convert_fusion.3
  430.1 4.0 convolution_convert_fusion.2
  434.2 4.5 multiply_convert_fusion
  438.7 4.0 convolution_convert_fusion.4
  442.7 4.2 multiply_convert_fusion.1
  446.9 6.2 fusion.55
  453.1 6.8 multiply_reduce_fusion
  464.3 5.5 collective-permute-start.40
  472.0 13.7 %attend_bwd.3 = bf16[1024,1152]{1,0:T(8,128)(2,1)S(1)} custom-call(s32[4]{0:T(128)S(1)} %get-tuple-element.52.low_ref, s32[4]{0:T(128)S(1)} %get-tuple-element.51.high_ref, bf16[1024,1152]{1,0:T(8,128)(2,1)S(1)} %convolution_convert_fusion.qkv_ref, bf16[1024,384]{1,0:T(8,128)(2,1)S(1)} %convolution_convert_fusion.8.dctx_ref, ...), custom_call_target="tpu_custom_call" | custom-call | flops 6442450944 | bytes 6451200 | tf_op jit(solution)/shard_map/attend_bwd/pallas_call | solution.py:177
  485.6 3.7 convolution_convert_fusion.6
  491.0 4.4 collective-permute-start.26
  495.4 13.9 %attend_bwd.2 = bf16[1024,1152]{1,0:T(8,128)(2,1)S(1)} custom-call(s32[4]{0:T(128)S(1)} %get-tuple-element.52.low_ref, s32[4]{0:T(128)S(1)} %get-tuple-element.51.high_ref, bf16[1024,1152]{1,0:T(8,128)(2,1)S(1)} %convolution_convert_fusion.1.qkv_ref, bf16[1024,384]{1,0:T(8,128)(2,1)S(1)} %convolution_convert_fusion.9.dctx_ref, ...), custom_call_target="tpu_custom_call" | custom-call | flops 6442450944 | bytes 6451200 | tf_op jit(solution)/shard_map/attend_bwd/pallas_call | solution.py:177
  509.3 4.6 fusion.8
  526.9 3.7 convolution_convert_fusion.7
  533.0 5.0 collective-permute-start.41
  544.3 4.2 add_convert_fusion.1
  548.5 3.6 collective-permute-done.41
  554.1 12.8 %collective-permute-done.42 = bf16[4,48,1536]{2,1,0:T(8,128)(2,1)S(1)} collective-permute-done((bf16[4,48,1536]{2,1,0:T(8,128)(2,1)S(1)}, bf16[4,48,1536]{2,1,0:T(8,128)(2,1)S(1)}, u32[]{:S(2)}, u32[]{:S(2)}) %collective-permute-start.42) | collective-permute-done | bytes 589856 | tf_op jit(solution)/shard_map/ppermute | solution.py:255
  567.7 9.7 %collective-permute-done.27 = bf16[4,48,1536]{2,1,0:T(8,128)(2,1)S(1)} collective-permute-done((bf16[4,48,1536]{2,1,0:T(8,128)(2,1)S(1)}, bf16[4,48,1536]{2,1,0:T(8,128)(2,1)S(1)}, u32[]{:S(2)}, u32[]{:S(2)}) %collective-permute-start.27) | collective-permute-done | bytes 589856 | tf_op jit(solution)/shard_map/ppermute | solution.py:255
  579.5 10.6 %collective-permute-done.28 = bf16[4,48,1536]{2,1,0:T(8,128)(2,1)S(1)} collective-permute-done((bf16[4,48,1536]{2,1,0:T(8,128)(2,1)S(1)}, bf16[4,48,1536]{2,1,0:T(8,128)(2,1)S(1)}, u32[]{:S(2)}, u32[]{:S(2)}) %collective-permute-start.28) | collective-permute-done | bytes 589856 | tf_op jit(solution)/shard_map/ppermute | solution.py:255
  594.6 8.2 %collective-permute-done.34 = bf16[4,48,1536]{2,1,0:T(8,128)(2,1)S(1)} collective-permute-done((bf16[4,48,1536]{2,1,0:T(8,128)(2,1)S(1)}, bf16[4,48,1536]{2,1,0:T(8,128)(2,1)S(1)}, u32[]{:S(2)}, u32[]{:S(2)}) %collective-permute-start.34) | collective-permute-done | bytes 589856 | tf_op jit(solution)/shard_map/ppermute | solution.py:255
  602.7 13.8 %collective-permute-done.35 = bf16[4,48,1536]{2,1,0:T(8,128)(2,1)S(1)} collective-permute-done((bf16[4,48,1536]{2,1,0:T(8,128)(2,1)S(1)}, bf16[4,48,1536]{2,1,0:T(8,128)(2,1)S(1)}, u32[]{:S(2)}, u32[]{:S(2)}) %collective-permute-start.35) | collective-permute-done | bytes 589856 | tf_op jit(solution)/shard_map/ppermute | solution.py:255
  616.6 3.7 collective-permute-start.32
  621.4 8.1 %collective-permute-done.31 = bf16[1,48,1536]{2,1,0:T(8,128)(2,1)S(1)} collective-permute-done((bf16[1,48,1536]{2,1,0:T(8,128)(2,1)S(1)}, bf16[1,48,1536]{2,1,0:T(8,128)(2,1)S(1)}, u32[]{:S(2)}, u32[]{:S(2)}) %collective-permute-start.31) | collective-permute-done | bytes 147488 | tf_op jit(solution)/shard_map/ppermute | solution.py:255
  632.2 8.1 %collective-permute-start.44 = (bf16[1,48,1536]{2,1,0:T(8,128)(2,1)}, bf16[1,48,1536]{2,1,0:T(8,128)(2,1)}, u32[]{:S(2)}, u32[]{:S(2)}) collective-permute-start(bf16[1,48,1536]{2,1,0:T(8,128)(2,1)} %get-tuple-element.94), channel_id=1, source_target_pairs={{0,8},{2,10},{4,12},{6,14},{8,0},{10,2},{12,4},{14,6},{16,24},{18,... | collective-permute-start | bytes 442376 | tf_op jit(solution)/shard_map/ppermute | solution.py:255
  646.2 6.0 collective-permute-done.45
  655.9 3.8 collective-permute-start.48
  665.6 3.7 collective-permute-start.51
  (294 shorter events, 122.8 us)
Async XLA Ops:
  3.7 8.9 %collective-permute-start.2 = (bf16[1,48,1536]{2,1,0:T(8,128)(2,1)S(1)}, bf16[1,48,1536]{2,1,0:T(8,128)(2,1)S(1)}, u32[]{:S(2)}, u32[]{:S(2)}) collective-permute-start(bf16[1,48,1536]{2,1,0:T(8,128)(2,1)S(1)} %maximum_bitcast_fusion.refs_0_), channel_id=1, source_target_pairs={{0,8},{2,10},{4,12},{6,14},{8,0},{10,2},{12,4},{14,6},{16,24},{18,... | collective-permute-start | bytes 442376 | tf_op jit(solution)/shard_map/ppermute | solution.py:255
  6.8 14.0 %collective-permute-start.3 = (bf16[1,48,1536]{2,1,0:T(8,128)(2,1)S(1)}, bf16[1,48,1536]{2,1,0:T(8,128)(2,1)S(1)}, u32[]{:S(2)}, u32[]{:S(2)}) collective-permute-start(bf16[1,48,1536]{2,1,0:T(8,128)(2,1)S(1)} %maximum_bitcast_fusion.refs_0_), channel_id=1, source_target_pairs={{0,16},{2,18},{4,20},{6,22},{8,24},{10,26},{12,28},{14,30},{16,0},... | collective-permute-start | bytes 442376 | tf_op jit(solution)/shard_map/ppermute | solution.py:255
  9.4 11.4 %collective-permute-start.4 = (bf16[1,48,1536]{2,1,0:T(8,128)(2,1)S(1)}, bf16[1,48,1536]{2,1,0:T(8,128)(2,1)S(1)}, u32[]{:S(2)}, u32[]{:S(2)}) collective-permute-start(bf16[1,48,1536]{2,1,0:T(8,128)(2,1)S(1)} %maximum_bitcast_fusion.refs_0_), channel_id=1, source_target_pairs={{0,24},{2,26},{4,28},{6,30},{8,16},{10,18},{12,20},{14,22},{16,8},... | collective-permute-start | bytes 442376 | tf_op jit(solution)/shard_map/ppermute | solution.py:255
  40.5 16.5 %collective-permute-start.5 = (bf16[4,48,1536]{2,1,0:T(8,128)(2,1)}, bf16[4,48,1536]{2,1,0:T(8,128)(2,1)S(1)}, u32[]{:S(2)}, u32[]{:S(2)}) collective-permute-start(bf16[4,48,1536]{2,1,0:T(8,128)(2,1)} %bitcast.146), channel_id=1, source_target_pairs={{0,2},{2,0},{4,6},{6,4},{8,10},{10,8},{12,14},{14,12},{16,18},{18,... | collective-permute-start | bytes 1769480 | tf_op jit(solution)/shard_map/ppermute | solution.py:255
  42.1 25.1 %collective-permute-start.6 = (bf16[4,48,1536]{2,1,0:T(8,128)(2,1)}, bf16[4,48,1536]{2,1,0:T(8,128)(2,1)S(1)}, u32[]{:S(2)}, u32[]{:S(2)}) collective-permute-start(bf16[4,48,1536]{2,1,0:T(8,128)(2,1)} %bitcast.147), channel_id=1, source_target_pairs={{0,4},{2,6},{4,0},{6,2},{8,12},{10,14},{12,8},{14,10},{16,20},{18,... | collective-permute-start | bytes 1769480 | tf_op jit(solution)/shard_map/ppermute | solution.py:255
  43.6 23.6 %collective-permute-start.7 = (bf16[4,48,1536]{2,1,0:T(8,128)(2,1)}, bf16[4,48,1536]{2,1,0:T(8,128)(2,1)S(1)}, u32[]{:S(2)}, u32[]{:S(2)}) collective-permute-start(bf16[4,48,1536]{2,1,0:T(8,128)(2,1)} %bitcast.148), channel_id=1, source_target_pairs={{0,6},{2,4},{4,2},{6,0},{8,14},{10,12},{12,10},{14,8},{16,22},{18,... | collective-permute-start | bytes 1769480 | tf_op jit(solution)/shard_map/ppermute | solution.py:255
  44.8 97.2 %collective-permute-start.10 = (bf16[1,48,1536]{2,1,0:T(8,128)(2,1)}, bf16[1,48,1536]{2,1,0:T(8,128)(2,1)}, u32[]{:S(2)}, u32[]{:S(2)}) collective-permute-start(bf16[1,48,1536]{2,1,0:T(8,128)(2,1)} %convert_bitcast_fusion.refs_0_), channel_id=1, source_target_pairs={{0,16},{2,18},{4,20},{6,22},{8,24},{10,26},{12,28},{14,30},{16,0},... | collective-permute-start | bytes 442376 | tf_op jit(solution)/shard_map/ppermute | solution.py:255
  48.0 97.6 %collective-permute-start.11 = (bf16[1,48,1536]{2,1,0:T(8,128)(2,1)}, bf16[1,48,1536]{2,1,0:T(8,128)(2,1)}, u32[]{:S(2)}, u32[]{:S(2)}) collective-permute-start(bf16[1,48,1536]{2,1,0:T(8,128)(2,1)} %convert_bitcast_fusion.refs_0_), channel_id=1, source_target_pairs={{0,24},{2,26},{4,28},{6,30},{8,16},{10,18},{12,20},{14,22},{16,8},... | collective-permute-start | bytes 442376 | tf_op jit(solution)/shard_map/ppermute | solution.py:255
  57.1 88.5 %collective-permute-start.9 = (bf16[1,48,1536]{2,1,0:T(8,128)(2,1)}, bf16[1,48,1536]{2,1,0:T(8,128)(2,1)}, u32[]{:S(2)}, u32[]{:S(2)}) collective-permute-start(bf16[1,48,1536]{2,1,0:T(8,128)(2,1)} %convert_bitcast_fusion.refs_0_), channel_id=1, source_target_pairs={{0,8},{2,10},{4,12},{6,14},{8,0},{10,2},{12,4},{14,6},{16,24},{18,... | collective-permute-start | bytes 442376 | tf_op jit(solution)/shard_map/ppermute | solution.py:255
  67.2 99.5 %collective-permute-start.1 = (f32[5,384]{1,0:T(8,128)S(1)}, f32[5,384]{1,0:T(8,128)S(1)}, u32[]{:S(2)}, u32[]{:S(2)}) collective-permute-start(f32[5,384]{1,0:T(8,128)S(1)} %pad_maximum_fusion.1), channel_id=1, source_target_pairs={{0,1},{1,0},{2,3},{3,2},{4,5},{5,4},{6,7},{7,6},{8,9},{9,8},{10,11... | collective-permute-start | bytes 23048 | tf_op jit(solution)/shard_map/ppermute | solution.py:255
  140.9 230.7 %collective-permute-start.8 = (bf16[768,1536]{1,0:T(8,128)(2,1)}, bf16[768,1536]{1,0:T(8,128)(2,1)}, u32[]{:S(2)}, u32[]{:S(2)}) collective-permute-start(bf16[768,1536]{1,0:T(8,128)(2,1)} %bitcast.150), channel_id=1, source_target_pairs={{0,1},{1,0},{2,3},{3,2},{4,5},{5,4},{6,7},{7,6},{8,9},{9,8},{10,11... | collective-permute-start | bytes 7077896 | tf_op jit(solution)/shard_map/ppermute | solution.py:255
  142.0 26.8 %collective-permute-start.15 = (bf16[1,48,1536]{2,1,0:T(8,128)(2,1)}, bf16[1,48,1536]{2,1,0:T(8,128)(2,1)S(1)}, u32[]{:S(2)}, u32[]{:S(2)}) collective-permute-start(bf16[1,48,1536]{2,1,0:T(8,128)(2,1)} %fusion.36.refs_0_), channel_id=1, source_target_pairs={{0,8},{2,10},{4,12},{6,14},{8,0},{10,2},{12,4},{14,6},{16,24},{18,... | collective-permute-start | bytes 442376 | tf_op jit(solution)/shard_map/ppermute | solution.py:255
  164.6 40.6 %collective-permute-start.12 = (bf16[4,48,1536]{2,1,0:T(8,128)(2,1)}, bf16[4,48,1536]{2,1,0:T(8,128)(2,1)}, u32[]{:S(2)}, u32[]{:S(2)}) collective-permute-start(bf16[4,48,1536]{2,1,0:T(8,128)(2,1)} %bitcast.138), channel_id=1, source_target_pairs={{0,2},{2,0},{4,6},{6,4},{8,10},{10,8},{12,14},{14,12},{16,18},{18,... | collective-permute-start | bytes 1769480 | tf_op jit(solution)/shard_map/ppermute | solution.py:255
  165.4 40.9 %collective-permute-start.13 = (bf16[4,48,1536]{2,1,0:T(8,128)(2,1)}, bf16[4,48,1536]{2,1,0:T(8,128)(2,1)}, u32[]{:S(2)}, u32[]{:S(2)}) collective-permute-start(bf16[4,48,1536]{2,1,0:T(8,128)(2,1)} %bitcast.139), channel_id=1, source_target_pairs={{0,4},{2,6},{4,0},{6,2},{8,12},{10,14},{12,8},{14,10},{16,20},{18,... | collective-permute-start | bytes 1769480 | tf_op jit(solution)/shard_map/ppermute | solution.py:255
  166.7 40.6 %collective-permute-start.14 = (bf16[4,48,1536]{2,1,0:T(8,128)(2,1)}, bf16[4,48,1536]{2,1,0:T(8,128)(2,1)}, u32[]{:S(2)}, u32[]{:S(2)}) collective-permute-start(bf16[4,48,1536]{2,1,0:T(8,128)(2,1)} %bitcast.140), channel_id=1, source_target_pairs={{0,6},{2,4},{4,2},{6,0},{8,14},{10,12},{12,10},{14,8},{16,22},{18,... | collective-permute-start | bytes 1769480 | tf_op jit(solution)/shard_map/ppermute | solution.py:255
  168.8 9.1 %collective-permute-start.16 = (bf16[1,48,1536]{2,1,0:T(8,128)(2,1)}, bf16[1,48,1536]{2,1,0:T(8,128)(2,1)S(1)}, u32[]{:S(2)}, u32[]{:S(2)}) collective-permute-start(bf16[1,48,1536]{2,1,0:T(8,128)(2,1)} %fusion.36.refs_0_), channel_id=1, source_target_pairs={{0,16},{2,18},{4,20},{6,22},{8,24},{10,26},{12,28},{14,30},{16,0},... | collective-permute-start | bytes 442376 | tf_op jit(solution)/shard_map/ppermute | solution.py:255
  185.5 172.1 %collective-permute-start = (bf16[1024,384]{1,0:T(8,128)(2,1)}, bf16[1024,384]{1,0:T(8,128)(2,1)}, u32[]{:S(2)}, u32[]{:S(2)}) collective-permute-start(bf16[1024,384]{1,0:T(8,128)(2,1)} %get-tuple-element.93), channel_id=1, source_target_pairs={{0,1},{1,0},{2,3},{3,2},{4,5},{5,4},{6,7},{7,6},{8,9},{9,8},{10,11... | collective-permute-start | bytes 2359304 | tf_op jit(solution)/shard_map/ppermute | solution.py:255
  205.2 78.2 %collective-permute-start.18 = (bf16[4,48,1536]{2,1,0:T(8,128)(2,1)}, bf16[4,48,1536]{2,1,0:T(8,128)(2,1)S(1)}, u32[]{:S(2)}, u32[]{:S(2)}) collective-permute-start(bf16[4,48,1536]{2,1,0:T(8,128)(2,1)} %bitcast.142), channel_id=1, source_target_pairs={{0,2},{2,0},{4,6},{6,4},{8,10},{10,8},{12,14},{14,12},{16,18},{18,... | collective-permute-start | bytes 1769480 | tf_op jit(solution)/shard_map/ppermute | solution.py:255
  206.3 77.2 %collective-permute-start.19 = (bf16[4,48,1536]{2,1,0:T(8,128)(2,1)}, bf16[4,48,1536]{2,1,0:T(8,128)(2,1)S(1)}, u32[]{:S(2)}, u32[]{:S(2)}) collective-permute-start(bf16[4,48,1536]{2,1,0:T(8,128)(2,1)} %bitcast.143), channel_id=1, source_target_pairs={{0,4},{2,6},{4,0},{6,2},{8,12},{10,14},{12,8},{14,10},{16,20},{18,... | collective-permute-start | bytes 1769480 | tf_op jit(solution)/shard_map/ppermute | solution.py:255
  207.3 77.5 %collective-permute-start.20 = (bf16[4,48,1536]{2,1,0:T(8,128)(2,1)}, bf16[4,48,1536]{2,1,0:T(8,128)(2,1)}, u32[]{:S(2)}, u32[]{:S(2)}) collective-permute-start(bf16[4,48,1536]{2,1,0:T(8,128)(2,1)} %bitcast.144), channel_id=1, source_target_pairs={{0,6},{2,4},{4,2},{6,0},{8,14},{10,12},{12,10},{14,8},{16,22},{18,... | collective-permute-start | bytes 1769480 | tf_op jit(solution)/shard_map/ppermute | solution.py:255
  283.4 138.6 %collective-permute-start.24 = (bf16[1024,384]{1,0:T(8,128)(2,1)}, bf16[1024,384]{1,0:T(8,128)(2,1)}, u32[]{:S(2)}, u32[]{:S(2)}) collective-permute-start(bf16[1024,384]{1,0:T(8,128)(2,1)} %get-tuple-element.88), channel_id=1, source_target_pairs={{0,1},{1,0},{2,3},{3,2},{4,5},{5,4},{6,7},{7,6},{8,9},{9,8},{10,11... | collective-permute-start | bytes 2359304 | tf_op jit(solution)/shard_map/ppermute | solution.py:255
  284.4 116.0 %collective-permute-start.21 = (bf16[768,1536]{1,0:T(8,128)(2,1)}, bf16[768,1536]{1,0:T(8,128)(2,1)}, u32[]{:S(2)}, u32[]{:S(2)}) collective-permute-start(bf16[768,1536]{1,0:T(8,128)(2,1)} %bitcast.131), channel_id=1, source_target_pairs={{0,1},{1,0},{2,3},{3,2},{4,5},{5,4},{6,7},{7,6},{8,9},{9,8},{10,11... | collective-permute-start | bytes 7077896 | tf_op jit(solution)/shard_map/ppermute | solution.py:255
  357.4 52.7 %collective-permute-start.22 = (bf16[768,1536]{1,0:T(8,128)(2,1)}, bf16[768,1536]{1,0:T(8,128)(2,1)}, u32[]{:S(2)}, u32[]{:S(2)}) collective-permute-start(bf16[768,1536]{1,0:T(8,128)(2,1)} %bitcast.155), channel_id=1, source_target_pairs={{0,1},{1,0},{2,3},{3,2},{4,5},{5,4},{6,7},{7,6},{8,9},{9,8},{10,11... | collective-permute-start | bytes 7077896 | tf_op jit(solution)/shard_map/ppermute | solution.py:255
  464.3 66.2 %collective-permute-start.40 = (bf16[768,1536]{1,0:T(8,128)(2,1)}, bf16[768,1536]{1,0:T(8,128)(2,1)}, u32[]{:S(2)}, u32[]{:S(2)}) collective-permute-start(bf16[768,1536]{1,0:T(8,128)(2,1)} %convolution_convert_fusion.2), channel_id=1, source_target_pairs={{0,1},{1,0},{2,3},{3,2},{4,5},{5,4},{6,7},{7,6},{8,9},{9,8},{10,11... | collective-permute-start | bytes 7077896 | tf_op jit(solution)/shard_map/ppermute | solution.py:255
  469.9 74.1 %collective-permute-start.33 = (bf16[768,1536]{1,0:T(8,128)(2,1)}, bf16[768,1536]{1,0:T(8,128)(2,1)}, u32[]{:S(2)}, u32[]{:S(2)}) collective-permute-start(bf16[768,1536]{1,0:T(8,128)(2,1)} %convolution_convert_fusion.4), channel_id=1, source_target_pairs={{0,1},{1,0},{2,3},{3,2},{4,5},{5,4},{6,7},{7,6},{8,9},{9,8},{10,11... | collective-permute-start | bytes 7077896 | tf_op jit(solution)/shard_map/ppermute | solution.py:255
  491.0 48.7 %collective-permute-start.26 = (bf16[768,1536]{1,0:T(8,128)(2,1)}, bf16[768,1536]{1,0:T(8,128)(2,1)}, u32[]{:S(2)}, u32[]{:S(2)}) collective-permute-start(bf16[768,1536]{1,0:T(8,128)(2,1)} %pad_maximum_fusion), channel_id=1, source_target_pairs={{0,1},{1,0},{2,3},{3,2},{4,5},{5,4},{6,7},{7,6},{8,9},{9,8},{10,11... | collective-permute-start | bytes 7077896 | tf_op jit(solution)/shard_map/ppermute | solution.py:255
  533.0 19.1 %collective-permute-start.41 = (bf16[4,48,1536]{2,1,0:T(8,128)(2,1)S(1)}, bf16[4,48,1536]{2,1,0:T(8,128)(2,1)S(1)}, u32[]{:S(2)}, u32[]{:S(2)}) collective-permute-start(bf16[4,48,1536]{2,1,0:T(8,128)(2,1)S(1)} %get-tuple-element.76), channel_id=1, source_target_pairs={{0,2},{2,0},{4,6},{6,4},{8,10},{10,8},{12,14},{14,12},{16,18},{18,... | collective-permute-start | bytes 1769480 | tf_op jit(solution)/shard_map/ppermute | solution.py:255
  538.0 28.8 %collective-permute-start.42 = (bf16[4,48,1536]{2,1,0:T(8,128)(2,1)S(1)}, bf16[4,48,1536]{2,1,0:T(8,128)(2,1)S(1)}, u32[]{:S(2)}, u32[]{:S(2)}) collective-permute-start(bf16[4,48,1536]{2,1,0:T(8,128)(2,1)S(1)} %get-tuple-element.78), channel_id=1, source_target_pairs={{0,4},{2,6},{4,0},{6,2},{8,12},{10,14},{12,8},{14,10},{16,20},{18,... | collective-permute-start | bytes 1769480 | tf_op jit(solution)/shard_map/ppermute | solution.py:255
  538.3 28.6 %collective-permute-start.43 = (bf16[4,48,1536]{2,1,0:T(8,128)(2,1)S(1)}, bf16[4,48,1536]{2,1,0:T(8,128)(2,1)S(1)}, u32[]{:S(2)}, u32[]{:S(2)}) collective-permute-start(bf16[4,48,1536]{2,1,0:T(8,128)(2,1)S(1)} %get-tuple-element.77), channel_id=1, source_target_pairs={{0,6},{2,4},{4,2},{6,0},{8,14},{10,12},{12,10},{14,8},{16,22},{18,... | collective-permute-start | bytes 1769480 | tf_op jit(solution)/shard_map/ppermute | solution.py:255
  542.1 35.4 %collective-permute-start.27 = (bf16[4,48,1536]{2,1,0:T(8,128)(2,1)S(1)}, bf16[4,48,1536]{2,1,0:T(8,128)(2,1)S(1)}, u32[]{:S(2)}, u32[]{:S(2)}) collective-permute-start(bf16[4,48,1536]{2,1,0:T(8,128)(2,1)S(1)} %get-tuple-element.82), channel_id=1, source_target_pairs={{0,2},{2,0},{4,6},{6,4},{8,10},{10,8},{12,14},{14,12},{16,18},{18,... | collective-permute-start | bytes 1769480 | tf_op jit(solution)/shard_map/ppermute | solution.py:255
  544.0 46.2 %collective-permute-start.28 = (bf16[4,48,1536]{2,1,0:T(8,128)(2,1)S(1)}, bf16[4,48,1536]{2,1,0:T(8,128)(2,1)S(1)}, u32[]{:S(2)}, u32[]{:S(2)}) collective-permute-start(bf16[4,48,1536]{2,1,0:T(8,128)(2,1)S(1)} %get-tuple-element.84), channel_id=1, source_target_pairs={{0,4},{2,6},{4,0},{6,2},{8,12},{10,14},{12,8},{14,10},{16,20},{18,... | collective-permute-start | bytes 1769480 | tf_op jit(solution)/shard_map/ppermute | solution.py:255
  552.1 39.8 %collective-permute-start.29 = (bf16[4,48,1536]{2,1,0:T(8,128)(2,1)S(1)}, bf16[4,48,1536]{2,1,0:T(8,128)(2,1)S(1)}, u32[]{:S(2)}, u32[]{:S(2)}) collective-permute-start(bf16[4,48,1536]{2,1,0:T(8,128)(2,1)S(1)} %get-tuple-element.83), channel_id=1, source_target_pairs={{0,6},{2,4},{4,2},{6,0},{8,14},{10,12},{12,10},{14,8},{16,22},{18,... | collective-permute-start | bytes 1769480 | tf_op jit(solution)/shard_map/ppermute | solution.py:255
  566.9 94.3 %collective-permute-start.25 = (bf16[1024,384]{1,0:T(8,128)(2,1)}, bf16[1024,384]{1,0:T(8,128)(2,1)}, u32[]{:S(2)}, u32[]{:S(2)}) collective-permute-start(bf16[1024,384]{1,0:T(8,128)(2,1)} %get-tuple-element.87), channel_id=1, source_target_pairs={{0,1},{1,0},{2,3},{3,2},{4,5},{5,4},{6,7},{7,6},{8,9},{9,8},{10,11... | collective-permute-start | bytes 2359304 | tf_op jit(solution)/shard_map/ppermute | solution.py:255
  566.9 104.8 %collective-permute-start.23 = (bf16[1024,384]{1,0:T(8,128)(2,1)}, bf16[1024,384]{1,0:T(8,128)(2,1)}, u32[]{:S(2)}, u32[]{:S(2)}) collective-permute-start(bf16[1024,384]{1,0:T(8,128)(2,1)} %get-tuple-element.91), channel_id=1, source_target_pairs={{0,1},{1,0},{2,3},{3,2},{4,5},{5,4},{6,7},{7,6},{8,9},{9,8},{10,11... | collective-permute-start | bytes 2359304 | tf_op jit(solution)/shard_map/ppermute | solution.py:255
  577.5 25.3 %collective-permute-start.34 = (bf16[4,48,1536]{2,1,0:T(8,128)(2,1)S(1)}, bf16[4,48,1536]{2,1,0:T(8,128)(2,1)S(1)}, u32[]{:S(2)}, u32[]{:S(2)}) collective-permute-start(bf16[4,48,1536]{2,1,0:T(8,128)(2,1)S(1)} %get-tuple-element.79), channel_id=1, source_target_pairs={{0,2},{2,0},{4,6},{6,4},{8,10},{10,8},{12,14},{14,12},{16,18},{18,... | collective-permute-start | bytes 1769480 | tf_op jit(solution)/shard_map/ppermute | solution.py:255
  590.2 26.4 %collective-permute-start.35 = (bf16[4,48,1536]{2,1,0:T(8,128)(2,1)S(1)}, bf16[4,48,1536]{2,1,0:T(8,128)(2,1)S(1)}, u32[]{:S(2)}, u32[]{:S(2)}) collective-permute-start(bf16[4,48,1536]{2,1,0:T(8,128)(2,1)S(1)} %get-tuple-element.81), channel_id=1, source_target_pairs={{0,4},{2,6},{4,0},{6,2},{8,12},{10,14},{12,8},{14,10},{16,20},{18,... | collective-permute-start | bytes 1769480 | tf_op jit(solution)/shard_map/ppermute | solution.py:255
  591.9 24.6 %collective-permute-start.36 = (bf16[4,48,1536]{2,1,0:T(8,128)(2,1)S(1)}, bf16[4,48,1536]{2,1,0:T(8,128)(2,1)S(1)}, u32[]{:S(2)}, u32[]{:S(2)}) collective-permute-start(bf16[4,48,1536]{2,1,0:T(8,128)(2,1)S(1)} %get-tuple-element.80), channel_id=1, source_target_pairs={{0,6},{2,4},{4,2},{6,0},{8,14},{10,12},{12,10},{14,8},{16,22},{18,... | collective-permute-start | bytes 1769480 | tf_op jit(solution)/shard_map/ppermute | solution.py:255
  602.7 18.7 %collective-permute-start.30 = (bf16[1,48,1536]{2,1,0:T(8,128)(2,1)S(1)}, bf16[1,48,1536]{2,1,0:T(8,128)(2,1)S(1)}, u32[]{:S(2)}, u32[]{:S(2)}) collective-permute-start(bf16[1,48,1536]{2,1,0:T(8,128)(2,1)S(1)} %get-tuple-element.100), channel_id=1, source_target_pairs={{0,8},{2,10},{4,12},{6,14},{8,0},{10,2},{12,4},{14,6},{16,24},{18,... | collective-permute-start | bytes 442376 | tf_op jit(solution)/shard_map/ppermute | solution.py:255
  616.6 12.9 %collective-permute-start.31 = (bf16[1,48,1536]{2,1,0:T(8,128)(2,1)S(1)}, bf16[1,48,1536]{2,1,0:T(8,128)(2,1)S(1)}, u32[]{:S(2)}, u32[]{:S(2)}) collective-permute-start(bf16[1,48,1536]{2,1,0:T(8,128)(2,1)S(1)} %get-tuple-element.102), channel_id=1, source_target_pairs={{0,16},{2,18},{4,20},{6,22},{8,24},{10,26},{12,28},{14,30},{16,0},... | collective-permute-start | bytes 442376 | tf_op jit(solution)/shard_map/ppermute | solution.py:255
  616.6 12.9 %collective-permute-start.32 = (bf16[1,48,1536]{2,1,0:T(8,128)(2,1)S(1)}, bf16[1,48,1536]{2,1,0:T(8,128)(2,1)S(1)}, u32[]{:S(2)}, u32[]{:S(2)}) collective-permute-start(bf16[1,48,1536]{2,1,0:T(8,128)(2,1)S(1)} %get-tuple-element.101), channel_id=1, source_target_pairs={{0,24},{2,26},{4,28},{6,30},{8,16},{10,18},{12,20},{14,22},{16,8},... | collective-permute-start | bytes 442376 | tf_op jit(solution)/shard_map/ppermute | solution.py:255
  621.4 10.8 %collective-permute-start.37 = (bf16[1,48,1536]{2,1,0:T(8,128)(2,1)}, bf16[1,48,1536]{2,1,0:T(8,128)(2,1)S(1)}, u32[]{:S(2)}, u32[]{:S(2)}) collective-permute-start(bf16[1,48,1536]{2,1,0:T(8,128)(2,1)} %get-tuple-element.97), channel_id=1, source_target_pairs={{0,8},{2,10},{4,12},{6,14},{8,0},{10,2},{12,4},{14,6},{16,24},{18,... | collective-permute-start | bytes 442376 | tf_op jit(solution)/shard_map/ppermute | solution.py:255
  629.5 10.8 %collective-permute-start.38 = (bf16[1,48,1536]{2,1,0:T(8,128)(2,1)}, bf16[1,48,1536]{2,1,0:T(8,128)(2,1)S(1)}, u32[]{:S(2)}, u32[]{:S(2)}) collective-permute-start(bf16[1,48,1536]{2,1,0:T(8,128)(2,1)} %get-tuple-element.99), channel_id=1, source_target_pairs={{0,16},{2,18},{4,20},{6,22},{8,24},{10,26},{12,28},{14,30},{16,0},... | collective-permute-start | bytes 442376 | tf_op jit(solution)/shard_map/ppermute | solution.py:255
  629.5 12.3 %collective-permute-start.39 = (bf16[1,48,1536]{2,1,0:T(8,128)(2,1)}, bf16[1,48,1536]{2,1,0:T(8,128)(2,1)}, u32[]{:S(2)}, u32[]{:S(2)}) collective-permute-start(bf16[1,48,1536]{2,1,0:T(8,128)(2,1)} %get-tuple-element.98), channel_id=1, source_target_pairs={{0,24},{2,26},{4,28},{6,30},{8,16},{10,18},{12,20},{14,22},{16,8},... | collective-permute-start | bytes 442376 | tf_op jit(solution)/shard_map/ppermute | solution.py:255
  632.2 14.0 %collective-permute-start.44 = (bf16[1,48,1536]{2,1,0:T(8,128)(2,1)}, bf16[1,48,1536]{2,1,0:T(8,128)(2,1)}, u32[]{:S(2)}, u32[]{:S(2)}) collective-permute-start(bf16[1,48,1536]{2,1,0:T(8,128)(2,1)} %get-tuple-element.94), channel_id=1, source_target_pairs={{0,8},{2,10},{4,12},{6,14},{8,0},{10,2},{12,4},{14,6},{16,24},{18,... | collective-permute-start | bytes 442376 | tf_op jit(solution)/shard_map/ppermute | solution.py:255
  640.3 11.9 %collective-permute-start.45 = (bf16[1,48,1536]{2,1,0:T(8,128)(2,1)}, bf16[1,48,1536]{2,1,0:T(8,128)(2,1)}, u32[]{:S(2)}, u32[]{:S(2)}) collective-permute-start(bf16[1,48,1536]{2,1,0:T(8,128)(2,1)} %get-tuple-element.96), channel_id=1, source_target_pairs={{0,16},{2,18},{4,20},{6,22},{8,24},{10,26},{12,28},{14,30},{16,0},... | collective-permute-start | bytes 442376 | tf_op jit(solution)/shard_map/ppermute | solution.py:255
  641.8 10.4 %collective-permute-start.46 = (bf16[1,48,1536]{2,1,0:T(8,128)(2,1)}, bf16[1,48,1536]{2,1,0:T(8,128)(2,1)}, u32[]{:S(2)}, u32[]{:S(2)}) collective-permute-start(bf16[1,48,1536]{2,1,0:T(8,128)(2,1)} %get-tuple-element.95), channel_id=1, source_target_pairs={{0,24},{2,26},{4,28},{6,30},{8,16},{10,18},{12,20},{14,22},{16,8},... | collective-permute-start | bytes 442376 | tf_op jit(solution)/shard_map/ppermute | solution.py:255
  655.9 8.2 %collective-permute-start.48 = (f32[32,128]{1,0:T(8,128)S(1)}, f32[32,128]{1,0:T(8,128)S(1)}, u32[]{:S(2)}, u32[]{:S(2)}) collective-permute-start(f32[32,128]{1,0:T(8,128)S(1)} %pad_add_fusion), channel_id=1, source_target_pairs={{0,2},{2,0},{4,6},{6,4},{8,10},{10,8},{12,14},{14,12},{16,18},{18,... | collective-permute-start | bytes 49160 | tf_op jit(solution)/shard_map/ppermute | solution.py:255
  665.6 9.1 %collective-permute-start.51 = (f32[32,128]{1,0:T(8,128)S(1)}, f32[32,128]{1,0:T(8,128)S(1)}, u32[]{:S(2)}, u32[]{:S(2)}) collective-permute-start(f32[32,128]{1,0:T(8,128)S(1)} %add_add_fusion.2), channel_id=1, source_target_pairs={{0,8},{2,10},{4,12},{6,14},{8,0},{10,2},{12,4},{14,6},{16,24},{18,... | collective-permute-start | bytes 49160 | tf_op jit(solution)/shard_map/ppermute | solution.py:255
  (66 other events, 1102.1 us)
